TPU v7x, 256 devices: a whole 4x4x8 slice. The times are simulated.
256 devices in a mesh: slab: 16 (over x, y), pencil: 16 (over z, core).
Axes of the slice: x: 4, y: 4, z: 8, core: 2. Of those that a mesh axis runs over, the one named last changes fastest.
Arguments:
- spec_vel: float32 [64, 1024, 2048], P('slab', None, 'pencil'), may hold values from -6 to 6
- shear_shift: int32 [64], P('slab'), may hold values from 0 to 1023
- patch_pos: int32 [16, 16, 3, 256], P('slab', 'pencil'), may hold values from 0 to 1008, as said below
- patch_count: int32 [16, 16], P('slab', 'pencil'), may hold values from 1 to 256, as said below
- interp_w: bfloat16 [16, 16, 64, 64, 256], P('slab', 'pencil'), may hold values from -0.75 to 0.75
- marker_vel: float32 [16, 16, 64, 256], P('slab', 'pencil'), may hold values from -6 to 6
Outputs:
- new_hat: float32 [64, 1024, 2048], P('slab', None, 'pencil')
- marker_force: float32 [16, 16, 64, 256], P('slab', 'pencil')
Inputs may be any that keep to these rules, and one draw needn't show every extreme that they name: `patch_pos`: rows of a slot: first plane below 4, and at most 0 on the last slab; cell along the second dimension below 64; first cell along the third dimension at most 1008, reached on every device. `patch_count`: some device has all 256 slots live.
All inputs are finite; a program needn't handle non-finite values.
Results may differ from a plain program's by a relative error of at most 0.0036.
Values may be sent and summed in bfloat16 or wider, within the bound.
No kernel may reach another device: no remote copies, remote signals or barrier semaphores. Data moves between devices by JAX's collectives and lax.ppermute only.
A program may use at most 64 MiB of HBM per device.

v0:
```python
import math

import jax
import jax.numpy as jnp
from jax import lax
from jax.sharding import PartitionSpec as P

PD = 4
PZ = 16


def from_behind(value, axis, by):
    size = lax.axis_size(axis)
    pairs = [(i, i + by) for i in range(size) if 0 <= i + by < size]
    return lax.ppermute(value, axis, pairs)


def dft_tables(length):
    steps_along = jnp.arange(length, dtype=jnp.int32)
    whole_turns = steps_along[:, None] * steps_along[None, :] % length
    angles = whole_turns.astype(jnp.float32) * (2.0 * math.pi / length)
    norming = 1.0 / math.sqrt(length)
    return (
        (jnp.cos(angles) * norming).astype(jnp.bfloat16),
        (jnp.sin(angles) * norming).astype(jnp.bfloat16),
    )


def depth_table(length):
    cosine, sines = dft_tables(length)
    return jnp.stack([cosine, -sines], axis=1).reshape(2 * length, length)


def rotate(values):
    parity = jnp.arange(values.shape[-1], dtype=jnp.int32) % 2
    forward = jnp.roll(values, -1, axis=-1)
    backward = jnp.roll(values, 1, axis=-1)
    return jnp.where(parity == 0, -forward, backward)


def shear_phase(spectral, shifts, first_wave, length):
    wave_ids = first_wave + jnp.arange(spectral.shape[-1], dtype=jnp.int32) // 2
    whole_turns = shifts[:, None] * wave_ids[None, :] % length
    angles = whole_turns.astype(jnp.float32) * (2.0 * math.pi / length)
    cosine = jnp.cos(angles)[:, None, :]
    sines = jnp.sin(angles)[:, None, :]
    return spectral * cosine + rotate(spectral) * sines


def viscous_factor(row_count, first_wave, wave_count, length):
    across = jnp.arange(row_count, dtype=jnp.int32)
    along_z = first_wave + jnp.arange(wave_count, dtype=jnp.int32)
    across_norm = jnp.minimum(across, row_count - across).astype(jnp.float32) / (row_count // 2)
    along_norm = jnp.minimum(along_z, length - along_z).astype(jnp.float32) / (length // 2)
    factor = 1.0 / (1.0 + across_norm[:, None] ** 2 + along_norm[None, :] ** 2)
    return jnp.repeat(factor, 2, axis=1)


def along_rows(table_cos, table_sin, values, sign_flip):
    direct = jnp.einsum("yk,xkm->xym", table_cos, values, preferred_element_type=jnp.float32)
    second = jnp.einsum("yk,xkm->xym", table_sin, values, preferred_element_type=jnp.float32)
    return direct + sign_flip * rotate(second)


def flat_index(plane, across, column, row_count, width):
    return (plane * row_count + across) * width + column


def shards(spec_vel, shear_shift, patch_pos, patch_count, interp_w, marker_vel):
    planes = spec_vel.shape[0]
    rows_all = spec_vel.shape[1]
    wave_count = spec_vel.shape[2] // 2
    length_z = wave_count * lax.axis_size("pencil")
    first_wave = lax.axis_index("pencil") * wave_count
    phased = shear_phase(spec_vel, shear_shift, first_wave, length_z)
    cosine_rows, sine_rows = dft_tables(rows_all)
    wave_table = depth_table(length_z)
    mixed_rows = along_rows(cosine_rows, sine_rows, phased.astype(jnp.bfloat16), 1.0).astype(
        jnp.bfloat16
    )
    velocity = jnp.einsum(
        "xym,mz->xyz",
        lax.all_to_all(mixed_rows, "pencil", split_axis=1, concat_axis=2, tiled=True),
        wave_table,
        preferred_element_type=jnp.float32,
    )
    row_count = velocity.shape[1]
    flat_vel = velocity.reshape(-1)
    positions = patch_pos[0, 0]
    live_count = patch_count[0, 0]
    weights = interp_w[0, 0]
    target = marker_vel[0, 0]
    cell_ids = jnp.arange(PD * PZ, dtype=jnp.int32)
    depth_step = (cell_ids // PZ)[:, None]
    span_step = (cell_ids % PZ)[:, None]
    plane_of = depth_step + positions[0][None, :]
    across = jnp.broadcast_to(positions[1][None, :], plane_of.shape)
    column = span_step + positions[2][None, :]
    inside = plane_of < planes
    index_in = flat_index(jnp.minimum(plane_of, planes - 1), across, column, row_count, length_z)
    upper_rim = from_behind(velocity[: PD - 1], "slab", -1)
    index_out = flat_index(jnp.maximum(plane_of - planes, 0), across, column, row_count, length_z)
    values = jnp.where(inside, flat_vel[index_in], upper_rim.reshape(-1)[index_out])
    interp = jnp.einsum(
        "mcp,cp->mp",
        weights,
        values,
        precision=lax.Precision.HIGHEST,
        preferred_element_type=jnp.float32,
    )
    live_slots = jnp.arange(weights.shape[2], dtype=jnp.int32)[None, :] < live_count
    forces = jnp.where(live_slots, target - interp, 0.0)
    spread = jnp.einsum(
        "mcp,mp->cp",
        weights,
        forces,
        precision=lax.Precision.HIGHEST,
        preferred_element_type=jnp.float32,
    )
    kept_part = jnp.where(inside, spread, 0.0)
    forcing_flat = jnp.zeros_like(flat_vel).at[index_in].add(kept_part)
    outer_part = jnp.where(inside, 0.0, spread)
    rim_flat = (
        jnp.zeros(((PD - 1) * row_count * length_z,), jnp.float32).at[index_out].add(outer_part)
    )
    lower_rim = from_behind(
        rim_flat.reshape(PD - 1, row_count, length_z).astype(jnp.bfloat16), "slab", 1
    ).astype(jnp.float32)
    forcing = forcing_flat.reshape(velocity.shape) + jnp.pad(
        lower_rim, ((0, planes - PD + 1), (0, 0), (0, 0))
    )
    source = forcing.astype(jnp.bfloat16)
    rows_hat = jnp.einsum(
        "xyz,mz->xym", source, wave_table, preferred_element_type=jnp.float32
    ).astype(jnp.bfloat16)
    wave_part = along_rows(
        cosine_rows,
        sine_rows,
        lax.all_to_all(rows_hat, "pencil", split_axis=2, concat_axis=1, tiled=True),
        -1.0,
    )
    new_hat = viscous_factor(rows_all, first_wave, wave_count, length_z)[None] * (
        phased + wave_part
    )
    return (new_hat, forces[None, None])


def solution(mesh):
    placed = (
        P("slab", None, "pencil"),
        P("slab"),
        P("slab", "pencil", None, None),
        P("slab", "pencil"),
        P("slab", "pencil", None, None, None),
        P("slab", "pencil", None, None),
    )
    return jax.shard_map(
        shards,
        mesh=mesh,
        in_specs=placed,
        out_specs=(P("slab", None, "pencil"), P("slab", "pencil", None, None)),
        check_vma=False,
    )
```

profile of v0, /device:TPU:7, one launch (start us, length us, event | category | flops | bytes accessed | tf_op | source)
XLA Modules:
  0.0 550.7 jit_solution(14586752876853217400)
XLA Ops:
  0.6 1.9 copy.67
  2.6 2.4 fusion.108
  5.1 2.8 fusion.17
  8.0 16.9 %fusion.34 = f32[4,1024,128]{1,2,0:T(8,128)S(1)} fusion(f32[4,1024,128]{1,2,0:T(8,128)S(1)} %fusion.17), kind=kOutput, calls=%fused_computation.51 | convolution fusion | flops 1091043328 | bytes 4194304 | tf_op jit(solution)/shard_map/yk,xkm->xym/dot_general | solution.py:61
  25.5 16.7 %fusion.20 = bf16[4,1024,128]{1,2,0:T(8,128)(2,1)S(1)} fusion(f32[4,1024,1]{1,2,0:T(1,128)S(1)} %get-tuple-element.19, f32[4,1024,127]{1,2,0:T(8,128)S(1)} %get-tuple-element.21, f32[4,1024,127]{1,2,0:T(8,128)S(1)} %get-tuple-element.20, f32[4,1024,1]{1,2,0:T(1,128)S(1)} %get-tuple-element.18, pred[128]{0:T(512)(128)(4,1)S(1)} %fusion.77, ...), kind=kOutput, calls=%fused_computation.40 | convolution fusion | flops 1094189056 | bytes 7340160 | tf_op jit(solution)/shard_map/yk,xkm->xym/dot_general | solution.py:60
  42.3 1.5 copy.72
  43.7 9.4 %all-to-all-start = ((bf16[4,1024,128]{2,0,1:T(4,128)(2,1)}), bf16[4,1024,128]{2,0,1:T(4,128)(2,1)S(1)}, u32[]{:S(2)}, u32[]{:S(2)}) async-start(bf16[4,1024,128]{2,0,1:T(4,128)(2,1)} %copy.72), calls=%async_computation | async-start | bytes 2097152 | tf_op jit(solution)/shard_map/all_to_all | solution.py:83
  53.2 15.7 %multiply_convert_fusion.1 = bf16[1024,1,1024]{2,0,1:T(8,128)(2,1)S(1)} fusion(), kind=kLoop, calls=%fused_computation.20 | loop fusion | flops 16777216 | bytes 2097152 | tf_op jit(solution)/shard_map/convert_element_type | solution.py:24
  68.9 15.8 %fusion.14 = bf16[1024,1,1024]{2,0,1:T(8,128)(2,1)S(1)} fusion(), kind=kLoop, calls=%fused_computation.32 | loop fusion | flops 19922944 | bytes 2097152 | tf_op jit(solution)/shard_map/neg | solution.py:31
  85.1 6.3 %copy.75 = bf16[1024,2,1024]{2,1,0:T(2,128)(2,1)} copy(bf16[1024,2,1024]{2,0,1:T(8,128)(2,1)S(1)} %pad_maximum_fusion) | data formatting | bytes 8388608 | tf_op jit(solution)/shard_map/stack | solution.py:31
  91.4 7.2 %reshape.578 = bf16[2048,1024,1]{1,0,2:T(8,128)(2,1)} reshape(bf16[1024,2,1024]{2,1,0:T(2,128)(2,1)} %copy.75) | data formatting | bytes 8388608 | tf_op jit(solution)/shard_map/reshape | solution.py:31
  99.7 3.5 fusion.40
  103.2 4.9 collective-permute-start
  108.4 90.7 %gather_fusion = f32[16384]{0:T(1024)S(1)} fusion(f32[262144]{0:T(1024)S(1)} %bitcast.102, s32[16384]{0:T(1024)S(1)} %broadcast_clamp_fusion.1), kind=kCustom, calls=%fused_computation | custom fusion | bytes 196608 | tf_op jit(solution)/shard_map/gather | solution.py:103
  199.4 90.5 %gather_fusion.1 = f32[16384]{0:T(1024)S(1)} fusion(f32[196608]{0:T(1024)S(1)} %bitcast.101, s32[16384]{0:T(1024)S(1)} %broadcast_clamp_fusion), kind=kCustom, calls=%fused_computation.1 | custom fusion | bytes 196608 | tf_op jit(solution)/shard_map/gather | solution.py:103
  290.0 0.7 multiply_reduce_fusion.1
  290.8 0.6 fusion.66
  292.1 86.0 %scatter_custom_fusion.1 = f32[196608]{0:T(1024)S(1)} fusion(s32[16384]{0:T(1024)S(1)} %bitcast.113, f32[16384]{0:T(1024)S(1)} %bitcast.115, f32[]{:T(128)} %constant.123.clone.1), kind=kCustom, calls=%fused_computation.62 | custom fusion | flops 16384 | bytes 786436 | tf_op jit(solution)/shard_map/scatter-add | solution.py:124
  378.3 1.9 collective-permute-start.1
  380.3 86.1 %scatter_custom_fusion = f32[262144]{0:T(1024)S(1)} fusion(s32[16384]{0:T(1024)S(1)} %bitcast.111, f32[16384]{0:T(1024)S(1)} %bitcast.114, f32[]{:T(128)} %constant.123.clone.1), kind=kCustom, calls=%fused_computation.60 | custom fusion | flops 16384 | bytes 1048580 | tf_op jit(solution)/shard_map/scatter-add | solution.py:121
  466.5 3.6 convolution_convert_fusion
  470.1 1.4 copy.76
  471.5 2.3 reshape.588
  473.8 7.5 %all-to-all-start.1 = ((bf16[16,2,16384]{2,1,0:T(2,128)(2,1)}), bf16[16,2,16384]{2,1,0:T(2,128)(2,1)S(1)}, u32[]{:S(2)}, u32[]{:S(2)}) async-start(bf16[16,2,16384]{2,1,0:T(2,128)(2,1)} %reshape.588), calls=%async_computation.1 | async-start | bytes 2097152 | tf_op jit(solution)/shard_map/all_to_all | solution.py:139
  481.6 1.2 mul.225
  482.8 26.4 %all-to-all-done.1 = bf16[16,2,16384]{2,1,0:T(2,128)(2,1)S(1)} async-done(((bf16[16,2,16384]{2,1,0:T(2,128)(2,1)}), bf16[16,2,16384]{2,1,0:T(2,128)(2,1)S(1)}, u32[]{:S(2)}, u32[]{:S(2)}) %all-to-all-start.1) | async-done | bytes 1048608 | tf_op jit(solution)/shard_map/all_to_all | solution.py:139
  509.2 1.3 reshape.589
  510.6 1.4 copy.97
  512.0 17.2 %fusion.37 = f32[4,1024,128]{1,2,0:T(8,128)S(1)} fusion(bf16[4,1024,128]{2,1,0:T(8,128)(2,1)S(1)} %bitcast.106), kind=kOutput, calls=%fused_computation.52 | convolution fusion | flops 1090519040 | bytes 3145728 | tf_op jit(solution)/shard_map/yk,xkm->xym/dot_general | solution.py:61
  529.8 0.9 copy-done.2
  530.8 17.9 %fusion.25 = f32[4,1024,128]{1,2,0:T(8,128)S(1)} fusion(f32[4,1024,128]{1,2,0:T(8,128)S(1)} %copy-done.2, f32[4,1024,1]{1,2,0:T(1,128)S(1)} %get-tuple-element.15, f32[4,1024,127]{1,2,0:T(8,128)S(1)} %get-tuple-element.17, f32[4,1024,127]{1,2,0:T(8,128)S(1)} %get-tuple-element.16, f32[4,1024,1]{1,2,0:T(1,128)S(1)} %get-tuple-element.14, ...), kind=kOutput, calls=%fused_computation.46 | convolution fusion | flops 1094713344 | bytes 9961600 | tf_op jit(solution)/shard_map/yk,xkm->xym/dot_general | solution.py:60
  548.7 1.8 copy.81
  (53 shorter events, 4.2 us)
Async XLA Ops:
  2.6 2.5 copy-start.7
  8.0 17.6 %copy-start.1 = (f32[4,1024,128]{1,2,0:T(8,128)}, f32[4,1024,128]{1,2,0:T(8,128)S(1)}, u32[]{:S(2)}) copy-start(f32[4,1024,128]{1,2,0:T(8,128)S(1)} %fusion.17) | copy-start | bytes 6291460
  43.7 55.8 %all-to-all-start = ((bf16[4,1024,128]{2,0,1:T(4,128)(2,1)}), bf16[4,1024,128]{2,0,1:T(4,128)(2,1)S(1)}, u32[]{:S(2)}, u32[]{:S(2)}) async-start(bf16[4,1024,128]{2,0,1:T(4,128)(2,1)} %copy.72), calls=%async_computation | async-start | bytes 2097152 | tf_op jit(solution)/shard_map/all_to_all | solution.py:83
  91.4 7.2 %copy-start.6 = (s32[1,1,3,256]{3,1,2,0:T(1,128)S(1)}, s32[1,1,3,256]{3,1,2,0:T(1,128)}, u32[]{:S(2)}) copy-start(s32[1,1,3,256]{3,1,2,0:T(1,128)} %param.8) | copy-start | bytes 9220
  103.2 96.0 %collective-permute-start = (f32[3,64,1024]{2,1,0:T(8,128)S(1)}, f32[3,64,1024]{2,1,0:T(8,128)S(1)}, u32[]{:S(2)}, u32[]{:S(2)}) collective-permute-start(f32[3,64,1024]{2,1,0:T(8,128)S(1)} %slice.83), channel_id=1, source_target_pairs={{16,0},{32,16},{48,32},{64,48},{80,64},{96,80},{112,96},{128,112},... | collective-permute-start | bytes 2359304 | tf_op jit(solution)/shard_map/ppermute | solution.py:15
  199.3 90.7 %copy-start = (bf16[1,1,64,64,256]{4,3,2,1,0:T(8,128)(2,1)S(1)}, bf16[1,1,64,64,256]{4,3,2,1,0:T(8,128)(2,1)}, u32[]{:S(2)}) copy-start(bf16[1,1,64,64,256]{4,3,2,1,0:T(8,128)(2,1)} %param.10) | copy-start | bytes 6291460
  199.4 91.4 %copy-start.5 = (f32[1,1,64,256]{3,2,1,0:T(8,128)S(1)}, f32[1,1,64,256]{3,2,1,0:T(8,128)}, u32[]{:S(2)}) copy-start(f32[1,1,64,256]{3,2,1,0:T(8,128)} %param.11) | copy-start | bytes 196612
  378.3 88.2 %collective-permute-start.1 = (bf16[3,64,1024]{2,1,0:T(8,128)(2,1)S(1)}, bf16[3,64,1024]{2,1,0:T(8,128)(2,1)}, u32[]{:S(2)}, u32[]{:S(2)}) collective-permute-start(bf16[3,64,1024]{2,1,0:T(8,128)(2,1)S(1)} %convert_element_type.112), channel_id=1, source_target_pairs={{0,16},{16,32},{32,48},{48,64},{64,80},{80,96},{96,112},{112,128},... | collective-permute-start | bytes 1179656 | tf_op jit(solution)/shard_map/ppermute | solution.py:15
  473.8 35.4 %all-to-all-start.1 = ((bf16[16,2,16384]{2,1,0:T(2,128)(2,1)}), bf16[16,2,16384]{2,1,0:T(2,128)(2,1)S(1)}, u32[]{:S(2)}, u32[]{:S(2)}) async-start(bf16[16,2,16384]{2,1,0:T(2,128)(2,1)} %reshape.588), calls=%async_computation.1 | async-start | bytes 2097152 | tf_op jit(solution)/shard_map/all_to_all | solution.py:139
  512.0 17.2 %copy-start.3 = (bf16[4,64,16,128]{3,1,2,0:T(8,128)(2,1)}, bf16[4,64,16,128]{3,1,2,0:T(8,128)(2,1)S(1)}, u32[]{:S(2)}) copy-start(bf16[4,64,16,128]{3,1,2,0:T(8,128)(2,1)S(1)} %copy.97) | copy-start | bytes 3145732
  529.1 1.6 copy-start.2
  529.2 1.7 copy-start.4
where the time goes:
time: 561 us; the launch traced here: 551 us
  local copies, waits for them, and re-layouts  213 us (38%)
  other arithmetic  209 us (37%)
  matrix products  75.8 us (14%)
  waiting for transfers between devices  26.4 us (5%)
  starting transfers between devices  23.8 us (4%)
    gather x2, local copies, waits for them, and re-layouts, shards(): flat_vel[index_in]  90.8 us
    gather x2, local copies, waits for them, and re-layouts, shards(): upper_rim.reshape(-1)[index_out]  90.6 us
    scatter-add x1, other arithmetic, shards(): forcing_flat = jnp.zeros_like(flat_vel).at[index_in].add(kept_part)  86.1 us
    scatter-add x1, other arithmetic, shards(): jnp.zeros(((PD - 1) * row_count * length_z,), jnp.float32).at[index_out]  86 us
    dot_general x2, matrix products, along_rows(): jnp.einsum('yk,xkm->xym', table_cos, values, preferred_element_type=jnp.f...  34.6 us
    dot_general x2, matrix products, along_rows(): jnp.einsum('yk,xkm->xym', table_sin, values, preferred_element_type=jnp.f...  34.1 us
    all_to_all x1, waiting for transfers between devices, shards(): lax.all_to_all(rows_hat, 'pencil', split_axis=2, concat_axis=1, tiled=True)  26.4 us
    neg x1, other arithmetic, depth_table(): return jnp.stack([cosine, -sines], axis=1).reshape(2 * length, length)  15.8 us
  transfers between devices with their start and end apart: 4, of which 1 were waited for; matrix products, arithmetic and copies ran while one was open for 41% of the time, Pallas kernels for 0%

commit v1 on v0

v1 whole, which is shorter than its diff:
```python
import functools
import math

import jax
import jax.numpy as jnp
import ml_dtypes
import numpy as np
from jax import lax
from jax.experimental import pallas as pl
from jax.experimental.pallas import tpu as pltpu
from jax.sharding import PartitionSpec as P

PD = 4
PZ = 16
MIB = 1 << 20
F32 = jnp.float32
BF16 = jnp.bfloat16


def dft_tables(length):
    steps = np.arange(length, dtype=np.int64)
    turns = steps[:, None] * steps[None, :] % length
    angles = turns.astype(np.float32) * np.float32(2.0 * math.pi / length)
    norming = np.float32(1.0 / math.sqrt(length))
    return np.cos(angles) * norming, np.sin(angles) * norming


@functools.cache
def row_table(length):
    cosine, sines = dft_tables(length)
    return np.concatenate([cosine, sines], axis=1).astype(ml_dtypes.bfloat16)


@functools.cache
def depth_table(length):
    cosine, sines = dft_tables(length)
    merged = np.stack([cosine, -sines], axis=1).reshape(2 * length, length)
    return merged.astype(ml_dtypes.bfloat16)


def turn_cos_sin(turns):
    x = turns * math.pi
    x2 = x * x
    s = x * (
        1.0
        + x2
        * (
            -1.0 / 6
            + x2
            * (1.0 / 120 + x2 * (-1.0 / 5040 + x2 * (1.0 / 362880 + x2 * (-1.0 / 39916800))))
        )
    )
    c = 1.0 + x2 * (
        -0.5
        + x2
        * (1.0 / 24 + x2 * (-1.0 / 720 + x2 * (1.0 / 40320 + x2 * (-1.0 / 3628800))))
    )
    return 1.0 - 2.0 * s * s, 2.0 * s * c


def wave_turns(product, length):
    half = length // 2
    return (((product + half) & (length - 1)) - half).astype(F32) * (1.0 / length)


def rotate(values):
    width = values.shape[-1]
    lane = lax.broadcasted_iota(jnp.int32, values.shape, values.ndim - 1)
    axis = values.ndim - 1
    ahead = pltpu.roll(values, width - 1, axis)
    behind = pltpu.roll(values, 1, axis)
    return jnp.where(lane % 2 == 0, -ahead, behind)


def plane_phase(shift, first_wave, width, length):
    lane = lax.broadcasted_iota(jnp.int32, (1, width), 1)
    return turn_cos_sin(wave_turns((first_wave + lane // 2) * shift, length))


def forward_body(length, scal, spec, table, out, basis):
    planes, rows, width = spec.shape
    step = pl.program_id(0)

    @pl.when(step == 0)
    def _():
        for x in range(planes):
            cosine, sines = plane_phase(scal[1 + x], scal[0], width, length)
            values = spec[x]
            turned = rotate(values)
            lanes = pl.ds(x * width, width)
            basis[pl.ds(0, rows), lanes] = (values * cosine + turned * sines).astype(BF16)
            basis[pl.ds(rows, rows), lanes] = (turned * cosine - values * sines).astype(BF16)

    mixed = jnp.dot(table[...], basis[...], preferred_element_type=F32).astype(BF16)
    dests, _, own, _ = out.shape
    for d in range(dests):
        for x in range(planes):
            out[d, x] = mixed[d * own : (d + 1) * own, x * width : (x + 1) * width]


def forward_rows(scal, spec, table, own, length):
    planes, rows, width = spec.shape
    steps = 4
    tile = rows // steps
    return pl.pallas_call(
        functools.partial(forward_body, length),
        grid=(steps,),
        in_specs=[
            pl.BlockSpec(memory_space=pltpu.SMEM),
            pl.BlockSpec((planes, rows, width), lambda i: (0, 0, 0)),
            pl.BlockSpec((tile, 2 * rows), lambda i: (i, 0)),
        ],
        out_specs=pl.BlockSpec((tile // own, planes, own, width), lambda i: (i, 0, 0, 0)),
        out_shape=jax.ShapeDtypeStruct((rows // own, planes, own, width), BF16),
        scratch_shapes=[pltpu.VMEM((2 * rows, planes * width), BF16)],
        compiler_params=pltpu.CompilerParams(vmem_limit_bytes=40 * MIB),
        cost_estimate=pl.CostEstimate(
            flops=4 * rows * rows * planes * width,
            bytes_accessed=4 * planes * rows * width + 4 * rows * rows + 2 * planes * rows * width,
            transcendentals=0,
        ),
        name="forward_rows",
    )(scal, spec, table)


def cells_body(slots, pos, coefs, table, own_out, above_out, field, own_cells, above_cells):
    step = pl.program_id(0)
    last = pl.num_programs(0) - 1
    sources, rows, width = coefs.shape
    span = rows // PD

    @pl.when(step == 0)
    def _():
        field[:, pl.ds(rows, rows), :] = jnp.zeros((field.shape[0], rows, 128), F32)
        field[field.shape[0] - 1, pl.ds(0, rows), :] = jnp.zeros((rows, 128), F32)

    left = jnp.concatenate([coefs[j] for j in range(sources)], axis=1)
    velocity = jnp.dot(left, table[...], preferred_element_type=F32)
    parts = velocity.shape[1] // 128
    for j in range(parts):
        field[parts * step + j, pl.ds(0, rows), :] = velocity[:, j * 128 : (j + 1) * 128]

    @pl.when(step == last)
    def _():
        lane = lax.broadcasted_iota(jnp.int32, (8, 128), 1)

        def take(p, base, offset, into):
            first = pos[base + p]
            across = pos[base + slots + p]
            start = pos[base + 2 * slots + p]
            tile = start // 128
            off = start % 128
            near = field[tile, pl.ds(across, 8, stride=span), :]
            far = field[tile + 1, pl.ds(across, 8, stride=span), :]
            both = jnp.where(lane >= off, near, far)
            both = pltpu.roll(both, 128 - off, 1)
            both = pltpu.roll(both, (offset - first) % 8, 0)
            into[pl.ds(pl.multiple_of(p * 8, 8), 8), :] = both

        def body(i, carry):
            for u in range(8):
                take(i * 8 + u, 0, 8, own_cells)
                take(i * 8 + u, 3 * slots, 4, above_cells)
            return carry

        lax.fori_loop(0, slots // 8, body, 0)
        wide = lax.broadcasted_iota(jnp.int32, (slots, 128), 1) < PZ
        total = jnp.zeros((slots, 128), F32)
        for a in range(PD):
            part = jnp.where(wide, own_cells[pl.ds(a, slots, stride=8), :], 0.0)
            total += part if a == 0 else pltpu.roll(part, a * PZ, 1)
        for a in range(1, PD):
            part = jnp.where(wide, above_cells[pl.ds(a, slots, stride=8), :], 0.0)
            total += pltpu.roll(part, PD * PZ + a * PZ, 1)
        turned = total.T
        own_out[...] = turned[: PD * PZ]
        above_out[...] = turned[PD * PZ + PZ :]


def patch_cells(pos, coefs, table, slots):
    sources, rows, width = coefs.shape
    length = table.shape[1]
    steps = 4
    tile = length // steps
    return pl.pallas_call(
        functools.partial(cells_body, slots),
        grid=(steps,),
        in_specs=[
            pl.BlockSpec(memory_space=pltpu.SMEM),
            pl.BlockSpec((sources, rows, width), lambda i: (0, 0, 0)),
            pl.BlockSpec((sources * width, tile), lambda i: (0, i)),
        ],
        out_specs=[
            pl.BlockSpec((PD * PZ, slots), lambda i: (0, 0)),
            pl.BlockSpec(((PD - 1) * PZ, slots), lambda i: (0, 0)),
        ],
        out_shape=[
            jax.ShapeDtypeStruct((PD * PZ, slots), F32),
            jax.ShapeDtypeStruct(((PD - 1) * PZ, slots), F32),
        ],
        scratch_shapes=[
            pltpu.VMEM((length // 128 + 1, 2 * rows, 128), F32),
            pltpu.VMEM((slots * 8, 128), F32),
            pltpu.VMEM((slots * 8, 128), F32),
        ],
        compiler_params=pltpu.CompilerParams(vmem_limit_bytes=40 * MIB),
        name="patch_cells",
    )(pos, coefs, table)


def force_body(count, weights, own, above, target, forces, own_out, up_out, values, spread):
    step = pl.program_id(0)
    markers, cells, slots = weights.shape

    @pl.when(step == 0)
    def _():
        values[pl.ds(0, PZ), :] = own[pl.ds(0, PZ), :]
        values[pl.ds(PZ, cells - PZ), :] = own[pl.ds(PZ, cells - PZ), :] + above[...]
        spread[...] = jnp.zeros((cells, slots), F32)

    live = lax.broadcasted_iota(jnp.int32, (1, slots), 1) < count[0]
    held = values[...]
    total = spread[...]
    for m in range(markers):
        wide = weights[m].astype(F32)
        interp = jnp.sum(wide * held, axis=0, keepdims=True)
        force = jnp.where(live, target[pl.ds(m, 1), :] - interp, 0.0)
        forces[pl.ds(m, 1), :] = force
        total = total + wide * force
    spread[...] = total

    @pl.when(step == pl.num_programs(0) - 1)
    def _():
        own_out[...] = total.astype(BF16)
        up_out[...] = total[PZ:].astype(BF16)


def marker_forces(count, weights, own, above, target):
    markers, cells, slots = weights.shape
    steps = 4
    tile = markers // steps
    whole = lambda i: (0, 0)
    return pl.pallas_call(
        force_body,
        grid=(steps,),
        in_specs=[
            pl.BlockSpec(memory_space=pltpu.SMEM),
            pl.BlockSpec((tile, cells, slots), lambda i: (i, 0, 0)),
            pl.BlockSpec((cells, slots), whole),
            pl.BlockSpec((cells - PZ, slots), whole),
            pl.BlockSpec((tile, slots), lambda i: (i, 0)),
        ],
        out_specs=[
            pl.BlockSpec((tile, slots), lambda i: (i, 0)),
            pl.BlockSpec((cells, slots), whole),
            pl.BlockSpec((cells - PZ, slots), whole),
        ],
        out_shape=[
            jax.ShapeDtypeStruct((markers, slots), F32),
            jax.ShapeDtypeStruct((cells, slots), BF16),
            jax.ShapeDtypeStruct((cells - PZ, slots), BF16),
        ],
        scratch_shapes=[pltpu.VMEM((cells, slots), F32), pltpu.VMEM((cells, slots), F32)],
        compiler_params=pltpu.CompilerParams(vmem_limit_bytes=32 * MIB),
        name="marker_forces",
    )(count, weights, own, above, target)


def spread_table(first_wave, width, length):
    row = jnp.arange(2 * width, dtype=jnp.int32)[:, None]
    cell = jnp.arange(PZ, dtype=jnp.int32)[None, :]
    wave = first_wave + (row % width) // 2
    angles = (wave * cell % length).astype(F32) * (2.0 * math.pi / length)
    norming = 1.0 / math.sqrt(length)
    cosine = jnp.cos(angles) * norming
    sines = jnp.sin(angles) * norming
    odd = row % 2 == 1
    straight = jnp.where(odd, -sines, cosine)
    quarter = jnp.where(odd, -cosine, -sines)
    entry = jnp.where(row < width, straight, quarter)
    high = entry.astype(BF16)
    low = (entry - high.astype(F32)).astype(BF16)
    blocks = 2 * PD - 1
    eye = jnp.eye(blocks, dtype=BF16)
    halves = [
        (eye[:, None, :, None] * part[None, :, None, :]).reshape(blocks * 2 * width, blocks * PZ)
        for part in (high, low)
    ]
    return jnp.concatenate(halves, axis=1)


def back_body(length, merge_steps, scal, spread, meta, turn, table, spec, out, basis):
    step = pl.program_id(0)
    planes, tile, width = out.shape
    rows = basis.shape[0] // 2
    group, _, slots = spread.shape
    own = rows // (group * merge_steps)

    @pl.when(step < merge_steps)
    def _():
        wave = scal[0] + lax.broadcasted_iota(jnp.int32, (width, 1), 0) // 2
        place = lax.broadcasted_iota(jnp.int32, (planes * own, slots), 0)
        for g in range(group):
            half = spread[g]
            doubled = jnp.concatenate([half, half], axis=0)
            sums = [jnp.zeros((own, width), F32) for _ in range(planes)]
            for side in range(2):
                start = meta[g, pl.ds(2 * side, 1), :]
                key = meta[g, pl.ds(2 * side + 1, 1), :]
                cosine, sines = turn_cos_sin(wave_turns(wave * start, length))
                hot = jnp.where(place == key, 1.0, 0.0).astype(BF16)
                depths = range(PD) if side == 0 else range(1, PD)
                for a in depths:
                    block = a if side == 0 else PD + a - 1
                    flat = jnp.dot(
                        turn[pl.ds(block * 2 * width, 2 * width), :],
                        doubled,
                        preferred_element_type=F32,
                    )
                    turned = (flat[:width] * cosine + flat[width:] * sines).astype(BF16)
                    if side == 0:
                        begin, count = 0, planes - a
                    else:
                        begin, count = PD - a, a
                    landed = lax.dot_general(
                        hot[begin * own : (begin + count) * own],
                        turned,
                        (((1,), (1,)), ((), ())),
                        preferred_element_type=F32,
                    )
                    for j in range(count):
                        x = begin + j + a - (0 if side == 0 else PD)
                        sums[x] = sums[x] + landed[j * own : (j + 1) * own]
            base = pl.multiple_of((step * group + g) * own, own)
            for x in range(planes):
                kept = sums[x].astype(BF16).astype(F32)
                lanes = pl.ds(x * width, width)
                basis[pl.ds(base, own), lanes] = kept.astype(BF16)
                basis[pl.ds(rows + base, own), lanes] = (-rotate(kept)).astype(BF16)

    @pl.when(step >= merge_steps)
    def _():
        mixed = jnp.dot(table[...], basis[...], preferred_element_type=F32)
        across = (step - merge_steps) * tile + lax.broadcasted_iota(jnp.int32, (tile, width), 0)
        along = scal[0] + lax.broadcasted_iota(jnp.int32, (tile, width), 1) // 2
        across_norm = jnp.minimum(across, rows - across).astype(F32) * (2.0 / rows)
        along_norm = jnp.minimum(along, length - along).astype(F32) * (2.0 / length)
        factor = 1.0 / (1.0 + across_norm * across_norm + along_norm * along_norm)
        for x in range(planes):
            cosine, sines = plane_phase(scal[1 + x], scal[0], width, length)
            values = spec[x]
            phased = values * cosine + rotate(values) * sines
            out[x] = factor * (phased + mixed[:, x * width : (x + 1) * width])


def back_rows(scal, spread, meta, turn, table, spec, length):
    planes, rows, width = spec.shape
    sources, cells, slots = spread.shape
    merge_steps = 4
    group = sources // merge_steps
    row_steps = 4
    tile = rows // row_steps
    merging = lambda i: (jnp.minimum(i, merge_steps - 1), 0, 0)
    later = lambda i: jnp.maximum(i - merge_steps, 0)
    return pl.pallas_call(
        functools.partial(back_body, length, merge_steps),
        grid=(merge_steps + row_steps,),
        in_specs=[
            pl.BlockSpec(memory_space=pltpu.SMEM),
            pl.BlockSpec((group, cells, slots), merging),
            pl.BlockSpec((group,) + meta.shape[1:], merging),
            pl.BlockSpec(turn.shape, lambda i: (0, 0)),
            pl.BlockSpec((tile, 2 * rows), lambda i: (later(i), 0)),
            pl.BlockSpec((planes, tile, width), lambda i: (0, later(i), 0)),
        ],
        out_specs=pl.BlockSpec((planes, tile, width), lambda i: (0, later(i), 0)),
        out_shape=jax.ShapeDtypeStruct((planes, rows, width), F32),
        scratch_shapes=[pltpu.VMEM((2 * rows, planes * width), BF16)],
        compiler_params=pltpu.CompilerParams(vmem_limit_bytes=48 * MIB),
        name="back_rows",
    )(scal, spread, meta, turn, table, spec)


def one_slab_on(value, by):
    size = lax.axis_size("slab")
    return lax.ppermute(value, "slab", [(i, i + by) for i in range(size) if 0 <= i + by < size])


def shards(spec_vel, shear_shift, patch_pos, patch_count, interp_w, marker_vel):
    planes, rows, width = spec_vel.shape
    pencils = lax.axis_size("pencil")
    own = rows // pencils
    length = width // 2 * pencils
    slots = patch_pos.shape[-1]
    first_wave = (lax.axis_index("pencil") * (width // 2)).astype(jnp.int32)
    scal = jnp.concatenate([first_wave[None], shear_shift])
    table = jnp.asarray(row_table(rows))

    positions = patch_pos[0, 0]
    behind = one_slab_on(positions, 1)
    coefs = forward_rows(scal, spec_vel, table, own, length)
    coefs = coefs.reshape(pencils, planes * own, width)
    here = lax.all_to_all(coefs, "pencil", split_axis=0, concat_axis=0, tiled=True)
    notes = jnp.stack(
        [
            positions[2],
            positions[0] * own + positions[1],
            behind[2],
            behind[0] * own + behind[1],
        ]
    )
    notes = jnp.concatenate([notes, jnp.zeros_like(notes)])[None]
    notes, _ = lax.optimization_barrier((notes, coefs))
    meta = lax.all_gather(notes, "pencil", axis=0, tiled=True)
    turn = spread_table(first_wave, width, length)

    flat_pos = jnp.concatenate([positions.reshape(-1), behind.reshape(-1)])
    values, above = patch_cells(flat_pos, here, jnp.asarray(depth_table(length)), slots)
    from_above = one_slab_on(above, -1)
    forces, spread, upward = marker_forces(
        patch_count[0], interp_w[0, 0], values, from_above, marker_vel[0, 0]
    )
    from_below = one_slab_on(upward, 1)
    message = jnp.concatenate([spread, from_below])[None]
    gathered = lax.all_gather(message, "pencil", axis=0, tiled=True)
    new_hat = back_rows(scal, gathered, meta, turn, table, spec_vel, length)
    return (new_hat, forces[None, None])


def solution(mesh):
    placed = (
        P("slab", None, "pencil"),
        P("slab"),
        P("slab", "pencil", None, None),
        P("slab", "pencil"),
        P("slab", "pencil", None, None, None),
        P("slab", "pencil", None, None),
    )
    return jax.shard_map(
        shards,
        mesh=mesh,
        in_specs=placed,
        out_specs=(P("slab", None, "pencil"), P("slab", "pencil", None, None)),
        check_vma=False,
    )
```

time: 561 us -> 128 us (0.23); the launches traced: 551 us -> 126 us
  other arithmetic: 209 us -> 1.43 us
  local copies, waits for them, and re-layouts: 213 us -> 8.34 us
  matrix products: 75.8 us -> 0 us
  Pallas kernels: 0 us -> 38.4 us
  blocking collectives: 0 us -> 33.2 us
    gather x4 -> x0, local copies, waits for them, and re-layouts: 181 us -> none  [the longest x2 90.8 us: shards(): flat_vel[index_in]]
    scatter-add x2 -> x0, other arithmetic: 172 us -> none  [the longest x1 86.1 us: shards(): forcing_flat = jnp.zeros_like(flat_vel).at[index_in].add(kept_part)]
    dot_general x6 -> x0, matrix products: 75.8 us -> none  [the longest x2 34.6 us: along_rows(): jnp.einsum('yk,xkm->xym', table_cos, values, preferred_element_type=jnp.f...]
    pallas_call x0 -> x4, Pallas kernels: none -> 38.4 us  [the longest x1 20.8 us: back_rows(): pl.pallas_call(functools.partial(back_body, length, merge_steps), grid=(m...]
    all_gather x0 -> x2, blocking collectives: none -> 33.2 us  [the longest x1 17.2 us: shards(): gathered = lax.all_gather(message, 'pencil', axis=0, tiled=True)]
    neg x1 -> x0, other arithmetic: 15.8 us -> none  [depth_table(): return jnp.stack([cosine, -sines], axis=1).reshape(2 * length, length)]
    convert_element_type x2, other arithmetic: 15.8 us -> 0.1 us  [the longest x1 0.09 us: spread_table(): high = entry.astype(BF16)]
    all_to_all x2 -> x1, starting transfers between devices: 16.9 us -> 9.3 us  [shards(): lax.all_to_all(coefs, 'pencil', split_axis=0, concat_axis=0, tiled=True)]
  transfers between devices with their start and end apart: 4 -> 4, of which waited for: 1 -> 3; matrix products, arithmetic and copies ran while one was open for 41% -> 1% of each run, Pallas kernels for 0% -> 0%
where the time goes in v1:
time: 128 us; the launch traced here: 126 us
  Pallas kernels  38.4 us (30%)
  blocking collectives  33.2 us (26%)
  waiting for transfers between devices  23.6 us (18%)
  starting transfers between devices  19.4 us (15%)
  local copies, waits for them, and re-layouts  8.34 us (7%)
  other arithmetic  1.43 us (1%)
  between operations  1.42 us (1%)
    all_to_all x1, waiting for transfers between devices, shards(): lax.all_to_all(coefs, 'pencil', split_axis=0, concat_axis=0, tiled=True)  21.1 us
    pallas_call x1, Pallas kernels, back_rows(): pl.pallas_call(functools.partial(back_body, length, merge_steps), grid=(m...  20.8 us
    all_gather x1, blocking collectives, shards(): gathered = lax.all_gather(message, 'pencil', axis=0, tiled=True)  17.2 us
    all_gather x1, blocking collectives, shards(): meta = lax.all_gather(notes, 'pencil', axis=0, tiled=True)  16 us
    ppermute x3, starting transfers between devices, one_slab_on(): lax.ppermute(value, 'slab', [(i, i + by) for i in range(size) if 0 <= i +...  10.1 us
    pallas_call x1, Pallas kernels, patch_cells(): pl.pallas_call(functools.partial(cells_body, slots), grid=(steps,), in_sp...  9.97 us
    all_to_all x1, starting transfers between devices, shards(): lax.all_to_all(coefs, 'pencil', split_axis=0, concat_axis=0, tiled=True)  9.3 us
    unnamed x17, local copies, waits for them, and re-layouts  7.75 us
  transfers between devices with their start and end apart: 4, of which 3 were waited for; matrix products, arithmetic and copies ran while one was open for 1% of the time, Pallas kernels for 0%

profile of v1, /device:TPU:7, one launch (start us, length us, event | category | flops | bytes accessed | tf_op | source)
XLA Modules:
  0.0 125.8 jit_solution(3862783800068212404)
XLA Ops:
  0.6 0.7 pad_add_fusion.1.scal
  1.4 0.0 copy-start.1
  1.4 2.2 %copy-done.1 = bf16[1024,2048]{1,0:T(8,128)(2,1)S(1)} copy-done((bf16[1024,2048]{1,0:T(8,128)(2,1)S(1)}, bf16[1024,2048]{1,0:T(8,128)(2,1)}, u32[]{:S(2)}) %copy-start.1) | copy-done | bytes 4194328
  3.6 0.0 copy-start.3
  3.6 1.6 %copy-done.3 = f32[4,1024,128]{2,1,0:T(8,128)S(1)} copy-done((f32[4,1024,128]{2,1,0:T(8,128)S(1)}, f32[4,1024,128]{2,1,0:T(8,128)}, u32[]{:S(2)}) %copy-start.3) | copy-done | bytes 2097176
  5.1 5.5 %forward_rows.1 = bf16[16,4,64,128]{3,2,1,0:T(8,128)(2,1)} custom-call(s32[5]{0:T(128)S(1)} %pad_add_fusion.1.scal, f32[4,1024,128]{2,1,0:T(8,128)S(1)} %copy-done.3, bf16[1024,2048]{1,0:T(8,128)(2,1)S(1)} %copy-done.1), custom_call_target="tpu_custom_call" | custom-call | flops 2147483648 | bytes 7340032 | tf_op jit(solution)/shard_map/forward_rows/pallas_call | solution.py:105
  10.7 0.0 copy-start.6
  10.7 9.3 %all-to-all-start = ((bf16[16,256,128]{2,1,0:T(8,128)(2,1)}), bf16[16,256,128]{2,1,0:T(8,128)(2,1)S(1)}, u32[]{:S(2)}, u32[]{:S(2)}) async-start(bf16[16,256,128]{2,1,0:T(8,128)(2,1)} %bitcast.3), calls=%async_computation | async-start | bytes 2097152 | tf_op jit(solution)/shard_map/all_to_all | solution.py:403
  20.0 0.0 copy-done.6
  20.0 3.2 %collective-permute-start = (s32[3,256]{1,0:T(4,128)S(1)}, s32[3,256]{1,0:T(4,128)S(1)}, u32[]{:S(2)}, u32[]{:S(2)}) collective-permute-start(s32[3,256]{1,0:T(4,128)S(1)} %bitcast.34), channel_id=1, source_target_pairs={{0,16},{16,32},{32,48},{48,64},{64,80},{80,96},{96,112},{112,128},... | collective-permute-start | bytes 9224 | tf_op jit(solution)/shard_map/ppermute | solution.py:386
  23.3 0.1 fusion.6
  23.4 0.1 broadcast_multiply_fusion.1
  23.5 0.1 copy.15
  23.6 0.1 copy.16
  23.7 0.3 copy.13
  24.0 0.3 copy.12
  24.3 0.4 pad_maximum_fusion.turn
  25.4 1.4 %collective-permute-done = s32[3,256]{1,0:T(4,128)S(1)} collective-permute-done((s32[3,256]{1,0:T(4,128)S(1)}, s32[3,256]{1,0:T(4,128)S(1)}, u32[]{:S(2)}, u32[]{:S(2)}) %collective-permute-start) | collective-permute-done | bytes 3104 | tf_op jit(solution)/shard_map/ppermute | solution.py:386
  26.8 21.1 %all-to-all-done.coefs = bf16[16,256,128]{2,1,0:T(8,128)(2,1)S(1)} async-done(((bf16[16,256,128]{2,1,0:T(8,128)(2,1)}), bf16[16,256,128]{2,1,0:T(8,128)(2,1)S(1)}, u32[]{:S(2)}, u32[]{:S(2)}) %all-to-all-start) | async-done | bytes 1048608 | tf_op jit(solution)/shard_map/all_to_all | solution.py:403
  47.9 2.2 %copy-done = bf16[2048,1024]{1,0:T(8,128)(2,1)S(1)} copy-done((bf16[2048,1024]{1,0:T(8,128)(2,1)S(1)}, bf16[2048,1024]{1,0:T(8,128)(2,1)}, u32[]{:S(2)}) %copy-start) | copy-done | bytes 4194328
  50.1 10.0 %patch_cells.1 = (f32[64,256]{1,0:T(8,128)S(1)}, f32[48,256]{1,0:T(8,128)S(1)}) custom-call(s32[1536]{0:T(1024)S(1)} %pad_add_fusion.pos, bf16[16,256,128]{2,1,0:T(8,128)(2,1)S(1)} %all-to-all-done.coefs, bf16[2048,1024]{1,0:T(8,128)(2,1)S(1)} %copy-done), custom_call_target="tpu_custom_call" | custom-call | tf_op jit(solution)/shard_map/patch_cells/pallas_call | solution.py:185
  60.1 4.9 %collective-permute-start.1 = (f32[48,256]{1,0:T(8,128)S(1)}, f32[48,256]{1,0:T(8,128)S(1)}, u32[]{:S(2)}, u32[]{:S(2)}) collective-permute-start(f32[48,256]{1,0:T(8,128)S(1)} %get-tuple-element.9), channel_id=1, source_target_pairs={{16,0},{32,16},{48,32},{64,48},{80,64},{96,80},{112,96},{128,112},... | collective-permute-start | bytes 147464 | tf_op jit(solution)/shard_map/ppermute | solution.py:386
  65.1 1.1 collective-permute-done.1.above
  66.2 0.0 copy-done.5
  66.2 1.6 %copy-done.2 = bf16[1,1,64,64,256]{4,3,2,1,0:T(8,128)(2,1)S(1)} copy-done((bf16[1,1,64,64,256]{4,3,2,1,0:T(8,128)(2,1)S(1)}, bf16[1,1,64,64,256]{4,3,2,1,0:T(8,128)(2,1)}, u32[]{:S(2)}) %copy-start.2) | copy-done | bytes 2097176
  67.8 2.0 %marker_forces.1 = (f32[64,256]{1,0:T(8,128)}, bf16[64,256]{1,0:T(8,128)(2,1)S(1)}, bf16[48,256]{1,0:T(8,128)(2,1)S(1)}) custom-call(s32[1]{0:T(128)} %bitcast.25.count, bf16[64,64,256]{2,1,0:T(8,128)(2,1)S(1)} %bitcast.27, f32[64,256]{1,0:T(8,128)S(1)} %get-tuple-element.8.own, f32[48,256]{1,0:T(8,128)S(1)} %collective-permute-done.1.above, ...), custom_call_target="tpu_custom_call" | custom-call | tf_op jit(solution)/shard_map/marker_forces/pallas_call | solution.py:243
  69.8 2.0 %collective-permute-start.2 = (bf16[48,256]{1,0:T(8,128)(2,1)S(1)}, bf16[48,256]{1,0:T(8,128)(2,1)S(1)}, u32[]{:S(2)}, u32[]{:S(2)}) collective-permute-start(bf16[48,256]{1,0:T(8,128)(2,1)S(1)} %get-tuple-element.11), channel_id=1, source_target_pairs={{0,16},{16,32},{32,48},{48,64},{64,80},{80,96},{96,112},{112,128},... | collective-permute-start | bytes 73736 | tf_op jit(solution)/shard_map/ppermute | solution.py:386
  71.8 16.0 %all_gather.7.meta = s32[16,8,256]{2,1,0:T(8,128)S(1)} all-gather(s32[1,8,256]{2,1,0:T(8,128)S(1)} %bitcast.33), channel_id=1, replica_groups=mesh['slab'=16,'pencil'=16] {'pencil'}, dimensions={0}, use_global_device_ids=true | all-gather | bytes 139264 | tf_op jit(solution)/shard_map/all_gather | solution.py:414
  87.8 0.0 collective-permute-done.2
  87.8 17.2 %all-gather = bf16[1792,256]{1,0:T(8,128)(2,1)S(1)} all-gather(bf16[112,256]{1,0:T(8,128)(2,1)S(1)} %pad_maximum_fusion.1), channel_id=2, replica_groups=mesh['slab'=16,'pencil'=16] {'pencil'}, dimensions={0}, use_global_device_ids=true | all-gather | bytes 974848 | tf_op jit(solution)/shard_map/all_gather | solution.py:425
  105.0 0.0 copy-done.4
  105.0 20.8 %back_rows.1 = f32[4,1024,128]{2,1,0:T(8,128)} custom-call(s32[5]{0:T(128)S(1)} %pad_add_fusion.1.scal, bf16[16,112,256]{2,1,0:T(8,128)(2,1)S(1)} %bitcast.26, s32[16,8,256]{2,1,0:T(8,128)S(1)} %all_gather.7.meta, bf16[1792,224]{1,0:T(8,128)(2,1)S(1)} %pad_maximum_fusion.turn, bf16[1024,2048]{1,0:T(8,128)(2,1)} %constant.71.clone.table, ...), custom_call_target="tpu_custom_call" | custom-call | tf_op jit(solution)/shard_map/back_rows/pallas_call | solution.py:365
  (17 shorter events, 0.1 us)
Async XLA Ops:
  1.4 2.2 %copy-start.1 = (bf16[1024,2048]{1,0:T(8,128)(2,1)S(1)}, bf16[1024,2048]{1,0:T(8,128)(2,1)}, u32[]{:S(2)}) copy-start(bf16[1024,2048]{1,0:T(8,128)(2,1)} %constant.71.clone.table) | copy-start | bytes 12582916
  3.6 1.6 %copy-start.3 = (f32[4,1024,128]{2,1,0:T(8,128)S(1)}, f32[4,1024,128]{2,1,0:T(8,128)}, u32[]{:S(2)}) copy-start(f32[4,1024,128]{2,1,0:T(8,128)} %spec.3) | copy-start | bytes 6291460
  10.7 9.3 %copy-start.6 = (s32[1,1,3,256]{3,1,2,0:T(1,128)S(1)}, s32[1,1,3,256]{3,1,2,0:T(1,128)}, u32[]{:S(2)}) copy-start(s32[1,1,3,256]{3,1,2,0:T(1,128)} %param.10) | copy-start | bytes 9220
  10.7 37.2 %all-to-all-start = ((bf16[16,256,128]{2,1,0:T(8,128)(2,1)}), bf16[16,256,128]{2,1,0:T(8,128)(2,1)S(1)}, u32[]{:S(2)}, u32[]{:S(2)}) async-start(bf16[16,256,128]{2,1,0:T(8,128)(2,1)} %bitcast.3), calls=%async_computation | async-start | bytes 2097152 | tf_op jit(solution)/shard_map/all_to_all | solution.py:403
  20.0 6.8 %collective-permute-start = (s32[3,256]{1,0:T(4,128)S(1)}, s32[3,256]{1,0:T(4,128)S(1)}, u32[]{:S(2)}, u32[]{:S(2)}) collective-permute-start(s32[3,256]{1,0:T(4,128)S(1)} %bitcast.34), channel_id=1, source_target_pairs={{0,16},{16,32},{32,48},{48,64},{64,80},{80,96},{96,112},{112,128},... | collective-permute-start | bytes 9224 | tf_op jit(solution)/shard_map/ppermute | solution.py:386
  47.9 2.2 %copy-start = (bf16[2048,1024]{1,0:T(8,128)(2,1)S(1)}, bf16[2048,1024]{1,0:T(8,128)(2,1)}, u32[]{:S(2)}) copy-start(bf16[2048,1024]{1,0:T(8,128)(2,1)} %constant.72.clone.table) | copy-start | bytes 12582916
  50.1 16.1 %copy-start.5 = (f32[1,1,64,256]{3,2,1,0:T(8,128)S(1)}, f32[1,1,64,256]{3,2,1,0:T(8,128)}, u32[]{:S(2)}) copy-start(f32[1,1,64,256]{3,2,1,0:T(8,128)} %param.13) | copy-start | bytes 196612
  60.1 6.1 %collective-permute-start.1 = (f32[48,256]{1,0:T(8,128)S(1)}, f32[48,256]{1,0:T(8,128)S(1)}, u32[]{:S(2)}, u32[]{:S(2)}) collective-permute-start(f32[48,256]{1,0:T(8,128)S(1)} %get-tuple-element.9), channel_id=1, source_target_pairs={{16,0},{32,16},{48,32},{64,48},{80,64},{96,80},{112,96},{128,112},... | collective-permute-start | bytes 147464 | tf_op jit(solution)/shard_map/ppermute | solution.py:386
  66.2 1.6 %copy-start.2 = (bf16[1,1,64,64,256]{4,3,2,1,0:T(8,128)(2,1)S(1)}, bf16[1,1,64,64,256]{4,3,2,1,0:T(8,128)(2,1)}, u32[]{:S(2)}) copy-start(bf16[1,1,64,64,256]{4,3,2,1,0:T(8,128)(2,1)} %param.12) | copy-start | bytes 6291460
  67.8 37.2 %copy-start.4 = (f32[4,1024,128]{2,1,0:T(8,128)S(1)}, f32[4,1024,128]{2,1,0:T(8,128)}, u32[]{:S(2)}) copy-start(f32[4,1024,128]{2,1,0:T(8,128)} %spec.3) | copy-start | bytes 6291460
  69.8 18.0 %collective-permute-start.2 = (bf16[48,256]{1,0:T(8,128)(2,1)S(1)}, bf16[48,256]{1,0:T(8,128)(2,1)S(1)}, u32[]{:S(2)}, u32[]{:S(2)}) collective-permute-start(bf16[48,256]{1,0:T(8,128)(2,1)S(1)} %get-tuple-element.11), channel_id=1, source_target_pairs={{0,16},{16,32},{32,48},{48,64},{64,80},{80,96},{96,112},{112,128},... | collective-permute-start | bytes 73736 | tf_op jit(solution)/shard_map/ppermute | solution.py:386

commit v2 on v1

v2 whole, which is shorter than its diff:
```python
import functools
import math

import jax
import jax.numpy as jnp
import ml_dtypes
import numpy as np
from jax import lax
from jax.experimental import pallas as pl
from jax.experimental.pallas import tpu as pltpu
from jax.sharding import PartitionSpec as P

PD = 4
PZ = 16
MIB = 1 << 20
VMEM_MIB = 56
PITCH = 9
FIELD_TILES = 9
FIELD_PLANES = 15
F32 = jnp.float32
BF16 = jnp.bfloat16


def dft_tables(length):
    steps = np.arange(length, dtype=np.int64)
    turns = steps[:, None] * steps[None, :] % length
    angles = turns.astype(np.float32) * np.float32(2.0 * math.pi / length)
    norming = np.float32(1.0 / math.sqrt(length))
    return np.cos(angles) * norming, np.sin(angles) * norming


@functools.cache
def row_table(length):
    cosine, sines = dft_tables(length)
    return np.concatenate([cosine, sines], axis=1).astype(ml_dtypes.bfloat16)


@functools.cache
def depth_table(length):
    cosine, sines = dft_tables(length)
    merged = np.stack([cosine, -sines], axis=1).reshape(2 * length, length)
    return merged.astype(ml_dtypes.bfloat16)


def turn_cos_sin(turns):
    x = turns * math.pi
    x2 = x * x
    s = x * (
        1.0
        + x2
        * (
            -1.0 / 6
            + x2
            * (1.0 / 120 + x2 * (-1.0 / 5040 + x2 * (1.0 / 362880 + x2 * (-1.0 / 39916800))))
        )
    )
    c = 1.0 + x2 * (
        -0.5
        + x2
        * (1.0 / 24 + x2 * (-1.0 / 720 + x2 * (1.0 / 40320 + x2 * (-1.0 / 3628800))))
    )
    return 1.0 - 2.0 * s * s, 2.0 * s * c


def wave_turns(product, length):
    half = length // 2
    return (((product + half) & (length - 1)) - half).astype(F32) * (1.0 / length)


def rotate(values):
    width = values.shape[-1]
    lane = lax.broadcasted_iota(jnp.int32, values.shape, values.ndim - 1)
    axis = values.ndim - 1
    ahead = pltpu.roll(values, width - 1, axis)
    behind = pltpu.roll(values, 1, axis)
    return jnp.where(lane % 2 == 0, -ahead, behind)


def plane_phase(shift, first_wave, width, length):
    lane = lax.broadcasted_iota(jnp.int32, (1, width), 1)
    return turn_cos_sin(wave_turns((first_wave + lane // 2) * shift, length))


def forward_body(length, prep_steps, scal, spec, table, out, basis):
    group, rows, width = spec.shape
    planes = group * prep_steps
    step = pl.program_id(0)
    for part in range(prep_steps):

        @pl.when(step == part)
        def _():
            for g in range(group):
                x = part * group + g
                cosine, sines = plane_phase(scal[1 + x], scal[0], width, length)
                values = spec[g]
                turned = rotate(values)
                lanes = pl.ds(x * width, width)
                basis[pl.ds(0, rows), lanes] = (values * cosine + turned * sines).astype(BF16)
                basis[pl.ds(rows, rows), lanes] = (turned * cosine - values * sines).astype(BF16)

    @pl.when(step >= prep_steps)
    def _():
        mixed = jnp.dot(table[...], basis[...], preferred_element_type=F32).astype(BF16)
        dests, _, own, _ = out.shape
        for d in range(dests):
            for x in range(planes):
                out[d, x] = mixed[d * own : (d + 1) * own, x * width : (x + 1) * width]


def forward_rows(scal, spec, table, own, length, prep_steps=2, row_steps=2):
    planes, rows, width = spec.shape
    tile = rows // row_steps
    later = lambda i: jnp.maximum(i - prep_steps, 0)
    return pl.pallas_call(
        functools.partial(forward_body, length, prep_steps),
        grid=(prep_steps + row_steps,),
        in_specs=[
            pl.BlockSpec(memory_space=pltpu.SMEM),
            pl.BlockSpec(
                (planes // prep_steps, rows, width),
                lambda i: (jnp.minimum(i, prep_steps - 1), 0, 0),
            ),
            pl.BlockSpec((tile, 2 * rows), lambda i: (later(i), 0)),
        ],
        out_specs=pl.BlockSpec((tile // own, planes, own, width), lambda i: (later(i), 0, 0, 0)),
        out_shape=jax.ShapeDtypeStruct((rows // own, planes, own, width), BF16),
        scratch_shapes=[pltpu.VMEM((2 * rows, planes * width), BF16)],
        compiler_params=pltpu.CompilerParams(vmem_limit_bytes=VMEM_MIB * MIB),
        cost_estimate=pl.CostEstimate(
            flops=4 * rows * rows * planes * width,
            bytes_accessed=4 * planes * rows * width + 4 * rows * rows + 2 * planes * rows * width,
            transcendentals=0,
        ),
        name="forward_rows",
    )(scal, spec, table)


def take_cells(spots, field, into, base, slots):
    lane = lax.broadcasted_iota(jnp.int32, (8, 128), 1)
    pitch = field.shape[0] // FIELD_TILES
    span = pitch // FIELD_PLANES
    batch = 16

    def body(i, carry):
        found = []
        for u in range(batch):
            spot = spots[base + i * batch + u]
            off = spots[base + slots + i * batch + u]
            near = field[pl.ds(spot, 8, stride=span), :]
            far = field[pl.ds(spot + pitch, 8, stride=span), :]
            found.append(pltpu.roll(jnp.where(lane >= off, near, far), 128 - off, 1))
        for u in range(batch):
            into[pl.ds((i * batch + u) * PITCH, 8), :] = found[u]
        return carry

    lax.fori_loop(0, slots // batch, body, 0)


def cells_first(into, slots):
    wide = lax.broadcasted_iota(jnp.int32, (slots, 128), 1) < PZ
    total = jnp.where(wide, into[pl.ds(0, slots, stride=PITCH), :], 0.0)
    for a in range(1, PD):
        part = jnp.where(wide, into[pl.ds(a, slots, stride=PITCH), :], 0.0)
        total += pltpu.roll(part, a * PZ, 1)
    return total.T


def above_body(slots, pos, coefs, table, field, above_out, into):
    step = pl.program_id(0)
    sources, rows, width = coefs.shape
    own = rows // PD
    span = own + 1
    pitch = FIELD_PLANES * span

    @pl.when(step == 0)
    def _():
        blank = jnp.zeros((PD * span, 128), F32)
        for t in range(FIELD_TILES):
            field[pl.ds(t * pitch, PD * span), :] = blank
            field[pl.ds(t * pitch + 2 * PD * span, (PD - 1) * span), :] = blank[span:]
        field[pl.ds((FIELD_TILES - 1) * pitch + PD * span, PD * span), :] = blank

    left = jnp.concatenate([coefs[j] for j in range(sources)], axis=1)
    velocity = jnp.dot(left, table[...], preferred_element_type=F32)
    parts = velocity.shape[1] // 128
    for j in range(parts):
        for x in range(PD):
            start = (parts * step + j) * pitch + (PD + x) * span
            field[pl.ds(start, own), :] = velocity[
                x * own : (x + 1) * own, j * 128 : (j + 1) * 128
            ]

    @pl.when(step == pl.num_programs(0) - 1)
    def _():
        take_cells(pos, field, into, 2 * slots, slots)
        above_out[...] = cells_first(into, slots)[PZ : PD * PZ]


def patch_spots(positions, behind, own):
    parts = []
    for held, lift in ((positions, PD), (behind, 0)):
        tile = held[2] // 128
        parts.append(
            (tile * FIELD_PLANES + held[0] + lift) * (own + 1) + held[1]
        )
        parts.append(held[2] % 128)
    return jnp.concatenate(parts)


def own_body(slots, pos, field, own_out, into):
    take_cells(pos, field, into, 0, slots)
    own_out[...] = cells_first(into, slots)[: PD * PZ]


def above_cells(pos, coefs, table, slots, steps=2):
    sources, rows, width = coefs.shape
    length = table.shape[1]
    span = rows // PD + 1
    tile = length // steps
    field_shape = (FIELD_TILES * FIELD_PLANES * span, 128)
    return pl.pallas_call(
        functools.partial(above_body, slots),
        grid=(steps,),
        in_specs=[
            pl.BlockSpec(memory_space=pltpu.SMEM),
            pl.BlockSpec((sources, rows, width), lambda i: (0, 0, 0)),
            pl.BlockSpec((sources * width, tile), lambda i: (0, i)),
        ],
        out_specs=[
            pl.BlockSpec(field_shape, lambda i: (0, 0)),
            pl.BlockSpec(((PD - 1) * PZ, slots), lambda i: (0, 0)),
        ],
        out_shape=[
            jax.ShapeDtypeStruct(field_shape, F32),
            jax.ShapeDtypeStruct(((PD - 1) * PZ, slots), F32),
        ],
        scratch_shapes=[pltpu.VMEM((slots * PITCH, 128), F32)],
        compiler_params=pltpu.CompilerParams(vmem_limit_bytes=VMEM_MIB * MIB),
        name="above_cells",
    )(pos, coefs, table)


def own_cells(pos, field, slots):
    return pl.pallas_call(
        functools.partial(own_body, slots),
        in_specs=[
            pl.BlockSpec(memory_space=pltpu.SMEM),
            pl.BlockSpec(memory_space=pltpu.VMEM),
        ],
        out_specs=pl.BlockSpec(memory_space=pltpu.VMEM),
        out_shape=jax.ShapeDtypeStruct((PD * PZ, slots), F32),
        scratch_shapes=[pltpu.VMEM((slots * PITCH, 128), F32)],
        compiler_params=pltpu.CompilerParams(vmem_limit_bytes=48 * MIB),
        name="own_cells",
    )(pos, field)


def force_body(count, weights, own, above, target, forces, own_out, up_out, values, spread):
    step = pl.program_id(0)
    markers, cells, slots = weights.shape

    @pl.when(step == 0)
    def _():
        values[pl.ds(0, PZ), :] = own[pl.ds(0, PZ), :]
        values[pl.ds(PZ, cells - PZ), :] = own[pl.ds(PZ, cells - PZ), :] + above[...]
        spread[...] = jnp.zeros((cells, slots), F32)

    live = lax.broadcasted_iota(jnp.int32, (1, slots), 1) < count[0]
    held = values[...]
    total = spread[...]
    for m in range(markers):
        wide = weights[m].astype(F32)
        interp = jnp.sum(wide * held, axis=0, keepdims=True)
        force = jnp.where(live, target[pl.ds(m, 1), :] - interp, 0.0)
        forces[pl.ds(m, 1), :] = force
        total = total + wide * force
    spread[...] = total

    @pl.when(step == pl.num_programs(0) - 1)
    def _():
        own_out[...] = total.astype(BF16)
        up_out[...] = total[PZ:].astype(BF16)


def marker_forces(count, weights, own, above, target):
    markers, cells, slots = weights.shape
    steps = 4
    tile = markers // steps
    whole = lambda i: (0, 0)
    return pl.pallas_call(
        force_body,
        grid=(steps,),
        in_specs=[
            pl.BlockSpec(memory_space=pltpu.SMEM),
            pl.BlockSpec((tile, cells, slots), lambda i: (i, 0, 0)),
            pl.BlockSpec((cells, slots), whole),
            pl.BlockSpec((cells - PZ, slots), whole),
            pl.BlockSpec((tile, slots), lambda i: (i, 0)),
        ],
        out_specs=[
            pl.BlockSpec((tile, slots), lambda i: (i, 0)),
            pl.BlockSpec((cells, slots), whole),
            pl.BlockSpec((cells - PZ, slots), whole),
        ],
        out_shape=[
            jax.ShapeDtypeStruct((markers, slots), F32),
            jax.ShapeDtypeStruct((cells, slots), BF16),
            jax.ShapeDtypeStruct((cells - PZ, slots), BF16),
        ],
        scratch_shapes=[pltpu.VMEM((cells, slots), F32), pltpu.VMEM((cells, slots), F32)],
        compiler_params=pltpu.CompilerParams(vmem_limit_bytes=32 * MIB),
        name="marker_forces",
    )(count, weights, own, above, target)


def spread_table(first_wave, width, length):
    half = width // 2
    row = jnp.arange(width, dtype=jnp.int32)[:, None]
    cell = jnp.arange(PZ, dtype=jnp.int32)[None, :]
    wave = first_wave + row % half
    cosine, sines = turn_cos_sin(wave_turns(wave * cell, length))
    entry = jnp.where(row < half, cosine, -sines) * (1.0 / math.sqrt(length))
    high = entry.astype(BF16)
    low = (entry - high.astype(F32)).astype(BF16)
    blocks = 2 * PD - 1
    eye = jnp.eye(blocks, dtype=BF16)
    halves = [
        (eye[:, None, :, None] * part[None, :, None, :]).reshape(blocks * width, blocks * PZ)
        for part in (high, low)
    ]
    return jnp.concatenate(halves, axis=1)


def lane_table(width):
    half = width // 2
    table = np.zeros((width, 2 * width), np.float32)
    for k in range(half):
        table[k, 2 * k] = 1.0
        table[half + k, 2 * k + 1] = 1.0
        table[half + k, width + 2 * k] = 1.0
        table[k, width + 2 * k + 1] = -1.0
    return table.astype(ml_dtypes.bfloat16)


def merge_sources(length, first_wave, parts, turn, own, planes, width):
    half = width // 2
    cells = (2 * PD - 1) * PZ
    slots = parts[0].shape[1]
    wave = first_wave + lax.broadcasted_iota(jnp.int32, (half, 1), 0)
    place = lax.broadcasted_iota(jnp.int32, (slots, planes * own), 1).astype(F32)
    low_half = lax.broadcasted_iota(jnp.int32, (width, 128), 1) < own
    held = jnp.concatenate([part[:cells] for part in parts], axis=1)
    flat = jnp.dot(turn, jnp.concatenate([held, held], axis=0), preferred_element_type=F32)
    ready = []
    for u, part in enumerate(parts):
        notes = part[cells:].astype(F32)
        keys = notes.T
        mine = flat[:, u * slots : (u + 1) * slots]
        for side in range(2):
            start = notes[3 * side : 3 * side + 1] * 32.0 + notes[3 * side + 1 : 3 * side + 2]
            cosine, sines = turn_cos_sin(wave_turns(wave * start.astype(jnp.int32), length))
            hot = jnp.where(place == keys[:, 3 * side + 2 : 3 * side + 3], 1.0, 0.0)
            turned = []
            for block in range(PD) if side == 0 else range(PD, 2 * PD - 1):
                real = mine[block * width : block * width + half]
                imag = mine[block * width + half : (block + 1) * width]
                turned.append((real * cosine + imag * sines).astype(BF16))
                turned.append((imag * cosine - real * sines).astype(BF16))
            ready.append((jnp.concatenate(turned, axis=0), hot.astype(BF16)))
    landed = [jnp.dot(left, hot, preferred_element_type=F32) for left, hot in ready]
    kept = []
    for u in range(len(parts)):
        mine = [landed[2 * u][a * width : (a + 1) * width] for a in range(PD)]
        below = [None] + [landed[2 * u + 1][a * width : (a + 1) * width] for a in range(PD - 1)]
        one = [mine[1][:, :128], jnp.where(low_half, mine[1][:, 128:], below[1][:, 128:])]
        two = [mine[2][:, :128], below[2][:, 128:]]
        three = [jnp.where(low_half, mine[3][:, :128], below[3][:, :128]), below[3][:, 128:]]
        odd = [pltpu.roll(one[0] + three[1], own, 1), pltpu.roll(one[1] + three[0], own, 1)]
        near = mine[0][:, :128] + two[1] + jnp.where(low_half, odd[1], odd[0])
        far = mine[0][:, 128:] + two[0] + jnp.where(low_half, odd[0], odd[1])
        kept.append(jnp.concatenate([near.T, far.T], axis=0).astype(BF16))
    return kept


def back_body(
    length, unroll, tiles,
    scal, spread, turn, lanes_of, table, spec, out,
    merged, basis, table_in, spec_in, out_from, sems, out_sems,
):
    planes, rows, width = spec_in.shape
    sources = spread.shape[0]
    own = rows // sources
    tile = rows // tiles
    loads = [
        pltpu.make_async_copy(table, table_in, sems.at[0]),
        pltpu.make_async_copy(spec, spec_in, sems.at[1]),
    ]
    for load in loads:
        load.start()

    def body(i, carry):
        parts = [spread[i * unroll + u] for u in range(unroll)]
        kept = merge_sources(length, scal[0], parts, turn[...], own, planes, width)
        for u in range(unroll):
            base = pl.multiple_of((i * unroll + u) * own, own)
            for x in range(planes):
                merged[x, pl.ds(base, own), :] = kept[u][x * own : (x + 1) * own]
        return carry

    lax.fori_loop(0, sources // unroll, body, 0)
    for x in range(planes):
        spaced = jnp.dot(merged[x], lanes_of[...], preferred_element_type=F32).astype(BF16)
        into = pl.ds(x * width, width)
        basis[pl.ds(0, rows), into] = spaced[:, :width]
        basis[pl.ds(rows, rows), into] = spaced[:, width:]
    for load in loads:
        load.wait()
    stores = []
    for t in range(tiles):
        span = pl.ds(t * tile, tile)
        mixed = jnp.dot(table_in[span, :], basis[...], preferred_element_type=F32)
        across = t * tile + lax.broadcasted_iota(jnp.int32, (tile, width), 0)
        along = scal[0] + lax.broadcasted_iota(jnp.int32, (tile, width), 1) // 2
        across_norm = jnp.minimum(across, rows - across).astype(F32) * (2.0 / rows)
        along_norm = jnp.minimum(along, length - along).astype(F32) * (2.0 / length)
        factor = 1.0 / (1.0 + across_norm * across_norm + along_norm * along_norm)
        for x in range(planes):
            cosine, sines = plane_phase(scal[1 + x], scal[0], width, length)
            values = spec_in[x, span, :]
            phased = values * cosine + rotate(values) * sines
            out_from[x, span, :] = factor * (phased + mixed[:, x * width : (x + 1) * width])
        store = pltpu.make_async_copy(out_from.at[:, span, :], out.at[:, span, :], out_sems.at[t])
        store.start()
        stores.append(store)
    for store in stores:
        store.wait()


def back_rows(scal, spread, turn, table, spec, length, unroll=8, tiles=4):
    planes, rows, width = spec.shape
    lanes_of = jnp.asarray(lane_table(width))
    whole = pl.BlockSpec(memory_space=pltpu.VMEM)
    away = pl.BlockSpec(memory_space=pl.ANY)
    return pl.pallas_call(
        functools.partial(back_body, length, unroll, tiles),
        in_specs=[pl.BlockSpec(memory_space=pltpu.SMEM), whole, whole, whole, away, away],
        out_specs=away,
        out_shape=jax.ShapeDtypeStruct((planes, rows, width), F32),
        scratch_shapes=[
            pltpu.VMEM((planes, rows, width), BF16),
            pltpu.VMEM((2 * rows, planes * width), BF16),
            pltpu.VMEM(table.shape, BF16),
            pltpu.VMEM(spec.shape, F32),
            pltpu.VMEM(spec.shape, F32),
            pltpu.SemaphoreType.DMA((2,)),
            pltpu.SemaphoreType.DMA((tiles,)),
        ],
        compiler_params=pltpu.CompilerParams(vmem_limit_bytes=VMEM_MIB * MIB),
        name="back_rows",
    )(scal, spread, turn, lanes_of, table, spec)


def one_slab_on(value, by):
    size = lax.axis_size("slab")
    return lax.ppermute(value, "slab", [(i, i + by) for i in range(size) if 0 <= i + by < size])


def shards(spec_vel, shear_shift, patch_pos, patch_count, interp_w, marker_vel):
    planes, rows, width = spec_vel.shape
    pencils = lax.axis_size("pencil")
    own = rows // pencils
    length = width // 2 * pencils
    slots = patch_pos.shape[-1]
    first_wave = (lax.axis_index("pencil") * (width // 2)).astype(jnp.int32)
    scal = jnp.concatenate([first_wave[None], shear_shift])
    table = jnp.asarray(row_table(rows))

    positions = patch_pos[0, 0]
    behind = one_slab_on(positions, 1)
    coefs = forward_rows(scal, spec_vel, table, own, length)
    coefs = coefs.reshape(pencils, planes * own, width)
    here = lax.all_to_all(coefs, "pencil", split_axis=0, concat_axis=0, tiled=True)
    notes = []
    for held in (positions, behind):
        notes += [held[2] // 32, held[2] % 32, held[0] * own + held[1]]
    notes = jnp.stack(notes + [jnp.zeros_like(notes[0])] * 2).astype(BF16)
    turn = spread_table(first_wave, width, length)
    here, turn, notes = lax.optimization_barrier((here, turn, notes))

    spots = patch_spots(positions, behind, own)
    field, above = above_cells(spots, here, jnp.asarray(depth_table(length)), slots)
    from_above = one_slab_on(above, -1)
    values = own_cells(spots, field, slots)
    forces, spread, upward = marker_forces(
        patch_count[0], interp_w[0, 0], values, from_above, marker_vel[0, 0]
    )
    from_below = one_slab_on(upward, 1)
    message = jnp.concatenate([spread, from_below, notes])[None]
    gathered = lax.all_gather(message, "pencil", axis=0, tiled=True)
    new_hat = back_rows(scal, gathered, turn, table, spec_vel, length)
    return (new_hat, forces[None, None])


def solution(mesh):
    placed = (
        P("slab", None, "pencil"),
        P("slab"),
        P("slab", "pencil", None, None),
        P("slab", "pencil"),
        P("slab", "pencil", None, None, None),
        P("slab", "pencil", None, None),
    )
    return jax.shard_map(
        shards,
        mesh=mesh,
        in_specs=placed,
        out_specs=(P("slab", None, "pencil"), P("slab", "pencil", None, None)),
        check_vma=False,
    )
```

time: 128 us -> 110 us (0.86); the launches traced: 126 us -> 109 us
  blocking collectives: 33.2 us -> 19.8 us
  Pallas kernels: 38.4 us -> 31.6 us
  waiting for transfers between devices: 23.6 us -> 30.3 us
  local copies, waits for them, and re-layouts: 8.34 us -> 4.38 us
  other arithmetic: 1.43 us -> 3.1 us
    all_gather x1 -> x0, blocking collectives: 16 us -> none  [shards(): meta = lax.all_gather(notes, 'pencil', axis=0, tiled=True)]
    pallas_call x3 -> x4, Pallas kernels: 36.3 us -> 29.5 us  [the longest x1 12.9 us: back_rows(): pl.pallas_call(functools.partial(back_body, length, unroll, tiles), in_sp...]
    all_to_all x1, waiting for transfers between devices: 21.1 us -> 25.6 us  [shards(): lax.all_to_all(coefs, 'pencil', split_axis=0, concat_axis=0, tiled=True)]
    unnamed x17 -> x15, local copies, waits for them, and re-layouts: 7.75 us -> 4 us
    all_gather x1, blocking collectives: 17.2 us -> 19.8 us  [shards(): gathered = lax.all_gather(message, 'pencil', axis=0, tiled=True)]
    ppermute x3, waiting for transfers between devices: 2.53 us -> 4.76 us  [one_slab_on(): lax.ppermute(value, 'slab', [(i, i + by) for i in range(size) if 0 <= i +...]
  transfers between devices with their start and end apart: 4 -> 4, of which waited for: 3 -> 2; matrix products, arithmetic and copies ran while one was open for 1% -> 3% of each run, Pallas kernels for 0% -> 9%
where the time goes in v2:
time: 110 us; the launch traced here: 109 us
  Pallas kernels  31.6 us (29%)
  waiting for transfers between devices  30.3 us (28%)
  blocking collectives  19.8 us (18%)
  starting transfers between devices  18.7 us (17%)
  local copies, waits for them, and re-layouts  4.38 us (4%)
  other arithmetic  3.1 us (3%)
  between operations  1.45 us (1%)
    all_to_all x1, waiting for transfers between devices, shards(): lax.all_to_all(coefs, 'pencil', split_axis=0, concat_axis=0, tiled=True)  25.6 us
    all_gather x1, blocking collectives, shards(): gathered = lax.all_gather(message, 'pencil', axis=0, tiled=True)  19.8 us
    pallas_call x1, Pallas kernels, back_rows(): pl.pallas_call(functools.partial(back_body, length, unroll, tiles), in_sp...  12.9 us
    all_to_all x1, starting transfers between devices, shards(): lax.all_to_all(coefs, 'pencil', split_axis=0, concat_axis=0, tiled=True)  9.43 us
    ppermute x3, starting transfers between devices, one_slab_on(): lax.ppermute(value, 'slab', [(i, i + by) for i in range(size) if 0 <= i +...  9.27 us
    pallas_call x1, Pallas kernels, above_cells(): pl.pallas_call(functools.partial(above_body, slots), grid=(steps,), in_sp...  7.29 us
    pallas_call x1, Pallas kernels, forward_rows(): pl.pallas_call(functools.partial(forward_body, length, prep_steps), grid=...  7.03 us
    ppermute x3, waiting for transfers between devices, one_slab_on(): lax.ppermute(value, 'slab', [(i, i + by) for i in range(size) if 0 <= i +...  4.76 us
  transfers between devices with their start and end apart: 4, of which 2 were waited for; matrix products, arithmetic and copies ran while one was open for 3% of the time, Pallas kernels for 9%

profile of v2, /device:TPU:7, one launch (start us, length us, event | category | flops | bytes accessed | tf_op | source)
XLA Modules:
  0.0 109.3 jit_solution(16223837936864539378)
XLA Ops:
  0.6 0.7 copy.21
  1.3 3.2 %collective-permute-start = (s32[3,256]{1,0:T(4,128)S(1)}, s32[3,256]{1,0:T(4,128)S(1)}, u32[]{:S(2)}, u32[]{:S(2)}) collective-permute-start(s32[3,256]{1,0:T(4,128)S(1)} %bitcast.61), channel_id=1, source_target_pairs={{0,16},{16,32},{32,48},{48,64},{64,80},{80,96},{96,112},{112,128},... | collective-permute-start | bytes 9224 | tf_op jit(solution)/shard_map/ppermute | solution.py:465
  4.5 1.3 %pad_add_fusion.1.scal = s32[5]{0:T(128)} fusion(s32[4]{0:T(128)} %param.10, s32[1]{0:T(128)} %bitcast), kind=kLoop, calls=%fused_computation.57 | loop fusion | flops 5 | bytes 40 | tf_op jit(solution)/shard_map/concatenate | solution.py:475
  5.8 0.0 copy-start.5
  5.8 7.0 %forward_rows.1 = bf16[16,4,64,128]{3,2,1,0:T(8,128)(2,1)} custom-call(s32[5]{0:T(128)} %pad_add_fusion.1.scal, f32[4,1024,128]{2,1,0:T(8,128)} %spec.3, bf16[1024,2048]{1,0:T(8,128)(2,1)} %constant.144.clone.table), custom_call_target="tpu_custom_call" | custom-call | flops 2147483648 | bytes 7340032 | tf_op jit(solution)/shard_map/forward_rows/pallas_call | solution.py:114
  12.8 9.4 %all-to-all-start = ((bf16[16,256,128]{2,1,0:T(8,128)(2,1)}), bf16[16,256,128]{2,1,0:T(8,128)(2,1)S(1)}, u32[]{:S(2)}, u32[]{:S(2)}) async-start(bf16[16,256,128]{2,1,0:T(8,128)(2,1)} %bitcast.50), calls=%async_computation | async-start | bytes 2097152 | tf_op jit(solution)/shard_map/all_to_all | solution.py:482
  22.3 0.1 broadcast_multiply_fusion.1
  22.5 0.2 copy.11
  22.7 0.2 copy.12
  22.9 0.0 copy-done.5
  22.9 1.0 pad_maximum_fusion.turn
  23.9 0.0 collective-permute-done
  24.0 0.6 pad_add_fusion.pos
  24.6 0.0 copy-start.3
  24.6 0.0 copy-start.1
  24.6 0.0 copy-start.2
  24.6 25.6 %all-to-all-done.coefs = bf16[16,256,128]{2,1,0:T(8,128)(2,1)S(1)} async-done(((bf16[16,256,128]{2,1,0:T(8,128)(2,1)}), bf16[16,256,128]{2,1,0:T(8,128)(2,1)S(1)}, u32[]{:S(2)}, u32[]{:S(2)}) %all-to-all-start) | async-done | bytes 1048608 | tf_op jit(solution)/shard_map/all_to_all | solution.py:482
  50.2 1.0 copy-done.4
  51.2 7.3 %above_cells.1 = (f32[8775,128]{1,0:T(8,128)}, f32[48,256]{1,0:T(8,128)}) custom-call(s32[1024]{0:T(1024)} %pad_add_fusion.pos, bf16[16,256,128]{2,1,0:T(8,128)(2,1)} %copy-done.4, bf16[2048,1024]{1,0:T(8,128)(2,1)} %constant.145.clone.table), custom_call_target="tpu_custom_call" | custom-call | tf_op jit(solution)/shard_map/above_cells/pallas_call | solution.py:221
  58.4 4.2 %collective-permute-start.1 = (f32[48,256]{1,0:T(8,128)}, f32[48,256]{1,0:T(8,128)S(1)}, u32[]{:S(2)}, u32[]{:S(2)}) collective-permute-start(f32[48,256]{1,0:T(8,128)} %get-tuple-element.12), channel_id=1, source_target_pairs={{16,0},{32,16},{48,32},{64,48},{80,64},{96,80},{112,96},{128,112},... | collective-permute-start | bytes 147464 | tf_op jit(solution)/shard_map/ppermute | solution.py:465
  63.3 0.0 copy-done.3
  63.3 0.0 copy-start
  63.3 2.3 %copy-done = f32[8775,128]{1,0:T(8,128)S(1)} copy-done((f32[8775,128]{1,0:T(8,128)S(1)}, f32[8775,128]{1,0:T(8,128)}, u32[]{:S(2)}) %copy-start) | copy-done | bytes 4492824
  65.6 2.3 %own_cells.1.own = f32[64,256]{1,0:T(8,128)S(1)} custom-call(s32[1024]{0:T(1024)S(1)} %copy-done.3, f32[8775,128]{1,0:T(8,128)S(1)} %copy-done), custom_call_target="tpu_custom_call" | custom-call | tf_op jit(solution)/shard_map/own_cells/pallas_call | solution.py:244
  67.9 0.0 collective-permute-done.1.above
  67.9 0.0 copy-done.1
  67.9 0.0 copy-done.2
  67.9 2.1 %marker_forces.1 = (f32[64,256]{1,0:T(8,128)}, bf16[64,256]{1,0:T(8,128)(2,1)S(1)}, bf16[48,256]{1,0:T(8,128)(2,1)S(1)}) custom-call(s32[1]{0:T(128)} %bitcast.46.count, bf16[64,64,256]{2,1,0:T(8,128)(2,1)S(1)} %bitcast.47, f32[64,256]{1,0:T(8,128)S(1)} %own_cells.1.own, f32[48,256]{1,0:T(8,128)S(1)} %collective-permute-done.1.above, f32[64,256]{1,0:T(8,128)S(1)} %bitcast.48), custom_call_target="tpu_custom_call" | custom-call | tf_op jit(solution)/shard_map/marker_forces/pallas_call | solution.py:290
  70.0 1.9 %collective-permute-start.2 = (bf16[48,256]{1,0:T(8,128)(2,1)S(1)}, bf16[48,256]{1,0:T(8,128)(2,1)S(1)}, u32[]{:S(2)}, u32[]{:S(2)}) collective-permute-start(bf16[48,256]{1,0:T(8,128)(2,1)S(1)} %get-tuple-element.14), channel_id=1, source_target_pairs={{0,16},{16,32},{32,48},{48,64},{64,80},{80,96},{96,112},{112,128},... | collective-permute-start | bytes 73736 | tf_op jit(solution)/shard_map/ppermute | solution.py:465
  71.9 4.8 %collective-permute-done.2 = bf16[48,256]{1,0:T(8,128)(2,1)S(1)} collective-permute-done((bf16[48,256]{1,0:T(8,128)(2,1)S(1)}, bf16[48,256]{1,0:T(8,128)(2,1)S(1)}, u32[]{:S(2)}, u32[]{:S(2)}) %collective-permute-start.2) | collective-permute-done | bytes 24608 | tf_op jit(solution)/shard_map/ppermute | solution.py:465
  76.7 19.8 %all-gather = bf16[1920,256]{1,0:T(8,128)(2,1)} all-gather(bf16[120,256]{1,0:T(8,128)(2,1)S(1)} %pad_maximum_fusion.1), channel_id=2, replica_groups=mesh['slab'=16,'pencil'=16] {'pencil'}, dimensions={0}, use_global_device_ids=true | all-gather | bytes 1044480 | tf_op jit(solution)/shard_map/all_gather | solution.py:499
  96.4 12.9 %back_rows.1 = f32[4,1024,128]{2,1,0:T(8,128)} custom-call(s32[5]{0:T(128)} %pad_add_fusion.1.scal, bf16[16,120,256]{2,1,0:T(8,128)(2,1)} %bitcast.49, bf16[896,224]{1,0:T(8,128)(2,1)} %pad_maximum_fusion.turn, bf16[128,256]{1,0:T(8,128)(2,1)} %constant.146.clone.lanes_of, bf16[1024,2048]{1,0:T(8,128)(2,1)} %constant.144.clone.table, f32[4,1024,128]{2,1,0:T(8,128)} %spec.3), custom_call_target="tpu_custom_call" | custom-call | tf_op jit(solution)/shard_map/back_rows/pallas_call | solution.py:444
  (16 shorter events, 0.2 us)
Async XLA Ops:
  1.3 22.6 %collective-permute-start = (s32[3,256]{1,0:T(4,128)S(1)}, s32[3,256]{1,0:T(4,128)S(1)}, u32[]{:S(2)}, u32[]{:S(2)}) collective-permute-start(s32[3,256]{1,0:T(4,128)S(1)} %bitcast.61), channel_id=1, source_target_pairs={{0,16},{16,32},{32,48},{48,64},{64,80},{80,96},{96,112},{112,128},... | collective-permute-start | bytes 9224 | tf_op jit(solution)/shard_map/ppermute | solution.py:465
  5.8 17.1 %copy-start.5 = (s32[1,1,3,256]{3,1,2,0:T(1,128)S(1)}, s32[1,1,3,256]{3,1,2,0:T(1,128)}, u32[]{:S(2)}) copy-start(s32[1,1,3,256]{3,1,2,0:T(1,128)} %param.11) | copy-start | bytes 9220
  12.8 37.4 %all-to-all-start = ((bf16[16,256,128]{2,1,0:T(8,128)(2,1)}), bf16[16,256,128]{2,1,0:T(8,128)(2,1)S(1)}, u32[]{:S(2)}, u32[]{:S(2)}) async-start(bf16[16,256,128]{2,1,0:T(8,128)(2,1)} %bitcast.50), calls=%async_computation | async-start | bytes 2097152 | tf_op jit(solution)/shard_map/all_to_all | solution.py:482
  24.6 38.7 %copy-start.3 = (s32[1024]{0:T(1024)S(1)}, s32[1024]{0:T(1024)}, u32[]{:S(2)}) copy-start(s32[1024]{0:T(1024)} %pad_add_fusion.pos) | copy-start | bytes 12292
  24.6 43.3 %copy-start.1 = (bf16[1,1,64,64,256]{4,3,2,1,0:T(8,128)(2,1)S(1)}, bf16[1,1,64,64,256]{4,3,2,1,0:T(8,128)(2,1)}, u32[]{:S(2)}) copy-start(bf16[1,1,64,64,256]{4,3,2,1,0:T(8,128)(2,1)} %param.13) | copy-start | bytes 6291460
  24.6 43.3 %copy-start.2 = (f32[1,1,64,256]{3,2,1,0:T(8,128)S(1)}, f32[1,1,64,256]{3,2,1,0:T(8,128)}, u32[]{:S(2)}) copy-start(f32[1,1,64,256]{3,2,1,0:T(8,128)} %param.14) | copy-start | bytes 196612
  50.2 1.0 copy-start.4
  58.4 9.4 %collective-permute-start.1 = (f32[48,256]{1,0:T(8,128)}, f32[48,256]{1,0:T(8,128)S(1)}, u32[]{:S(2)}, u32[]{:S(2)}) collective-permute-start(f32[48,256]{1,0:T(8,128)} %get-tuple-element.12), channel_id=1, source_target_pairs={{16,0},{32,16},{48,32},{64,48},{80,64},{96,80},{112,96},{128,112},... | collective-permute-start | bytes 147464 | tf_op jit(solution)/shard_map/ppermute | solution.py:465
  63.3 2.3 %copy-start = (f32[8775,128]{1,0:T(8,128)S(1)}, f32[8775,128]{1,0:T(8,128)}, u32[]{:S(2)}) copy-start(f32[8775,128]{1,0:T(8,128)} %get-tuple-element.11.field) | copy-start | bytes 13478404
  70.0 6.7 %collective-permute-start.2 = (bf16[48,256]{1,0:T(8,128)(2,1)S(1)}, bf16[48,256]{1,0:T(8,128)(2,1)S(1)}, u32[]{:S(2)}, u32[]{:S(2)}) collective-permute-start(bf16[48,256]{1,0:T(8,128)(2,1)S(1)} %get-tuple-element.14), channel_id=1, source_target_pairs={{0,16},{16,32},{32,48},{48,64},{64,80},{80,96},{96,112},{112,128},... | collective-permute-start | bytes 73736 | tf_op jit(solution)/shard_map/ppermute | solution.py:465

commit v3 on v2

--- a/solution.py
+++ b/solution.py
@@ -81,58 +81,87 @@
     return turn_cos_sin(wave_turns((first_wave + lane // 2) * shift, length))
 
 
-def forward_body(length, prep_steps, scal, spec, table, out, basis):
-    group, rows, width = spec.shape
-    planes = group * prep_steps
-    step = pl.program_id(0)
-    for part in range(prep_steps):
-
-        @pl.when(step == part)
-        def _():
-            for g in range(group):
-                x = part * group + g
-                cosine, sines = plane_phase(scal[1 + x], scal[0], width, length)
-                values = spec[g]
-                turned = rotate(values)
-                lanes = pl.ds(x * width, width)
-                basis[pl.ds(0, rows), lanes] = (values * cosine + turned * sines).astype(BF16)
-                basis[pl.ds(rows, rows), lanes] = (turned * cosine - values * sines).astype(BF16)
-
-    @pl.when(step >= prep_steps)
-    def _():
-        mixed = jnp.dot(table[...], basis[...], preferred_element_type=F32).astype(BF16)
-        dests, _, own, _ = out.shape
-        for d in range(dests):
+def forward_body(
+    length, tiles, first, shifts, spec, table, out,
+    basis, spec_in, table_in, out_from, sems, table_sems, out_sems,
+):
+    planes, rows, width = spec_in.shape
+    dests, _, own, _ = out_from.shape
+    tile = rows // tiles
+    loads = [pltpu.make_async_copy(spec.at[x], spec_in.at[x], sems.at[x]) for x in range(planes)]
+    spans = [pl.ds(t * tile, tile) for t in range(tiles)]
+    tables = [
+        pltpu.make_async_copy(table.at[span, :], table_in.at[span, :], table_sems.at[t])
+        for t, span in enumerate(spans)
+    ]
+    for load in loads + tables:
+        load.start()
+    for x in range(planes):
+        loads[x].wait()
+        cosine, sines = plane_phase(shifts[x], first[0], width, length)
+        values = spec_in[x]
+        turned = rotate(values)
+        lanes = pl.ds(x * width, width)
+        basis[pl.ds(0, rows), lanes] = (values * cosine + turned * sines).astype(BF16)
+        basis[pl.ds(rows, rows), lanes] = (turned * cosine - values * sines).astype(BF16)
+    stores = []
+    group = dests // tiles
+    for t, span in enumerate(spans):
+        tables[t].wait()
+        mixed = jnp.dot(table_in[span, :], basis[...], preferred_element_type=F32).astype(BF16)
+        for d in range(group):
             for x in range(planes):
-                out[d, x] = mixed[d * own : (d + 1) * own, x * width : (x + 1) * width]
-
-
-def forward_rows(scal, spec, table, own, length, prep_steps=2, row_steps=2):
+                out_from[t * group + d, x] = mixed[
+                    d * own : (d + 1) * own, x * width : (x + 1) * width
+                ]
+        ready = pl.ds(t * group, group)
+        store = pltpu.make_async_copy(out_from.at[ready], out.at[ready], out_sems.at[t])
+        store.start()
+        stores.append(store)
+    for store in stores:
+        store.wait()
+
+
+def forward_rows(first, shifts, spec, table, own, length, tiles=2):
     planes, rows, width = spec.shape
-    tile = rows // row_steps
-    later = lambda i: jnp.maximum(i - prep_steps, 0)
+    small = pl.BlockSpec(memory_space=pltpu.SMEM)
+    away = pl.BlockSpec(memory_space=pl.ANY)
+    shape = (rows // own, planes, own, width)
     return pl.pallas_call(
-        functools.partial(forward_body, length, prep_steps),
-        grid=(prep_steps + row_steps,),
-        in_specs=[
-            pl.BlockSpec(memory_space=pltpu.SMEM),
-            pl.BlockSpec(
-                (planes // prep_steps, rows, width),
-                lambda i: (jnp.minimum(i, prep_steps - 1), 0, 0),
-            ),
-            pl.BlockSpec((tile, 2 * rows), lambda i: (later(i), 0)),
-        ],
-        out_specs=pl.BlockSpec((tile // own, planes, own, width), lambda i: (later(i), 0, 0, 0)),
-        out_shape=jax.ShapeDtypeStruct((rows // own, planes, own, width), BF16),
-        scratch_shapes=[pltpu.VMEM((2 * rows, planes * width), BF16)],
+        functools.partial(forward_body, length, tiles),
+        in_specs=[small, small, away, away],
+        out_specs=away,
+        out_shape=jax.ShapeDtypeStruct(shape, BF16),
+        scratch_shapes=[
+            pltpu.VMEM((2 * rows, planes * width), BF16),
+            pltpu.VMEM(spec.shape, F32),
+            pltpu.VMEM(table.shape, BF16),
+            pltpu.VMEM(shape, BF16),
+            pltpu.SemaphoreType.DMA((planes,)),
+            pltpu.SemaphoreType.DMA((tiles,)),
+            pltpu.SemaphoreType.DMA((tiles,)),
+        ],
         compiler_params=pltpu.CompilerParams(vmem_limit_bytes=VMEM_MIB * MIB),
-        cost_estimate=pl.CostEstimate(
-            flops=4 * rows * rows * planes * width,
-            bytes_accessed=4 * planes * rows * width + 4 * rows * rows + 2 * planes * rows * width,
-            transcendentals=0,
-        ),
         name="forward_rows",
-    )(scal, spec, table)
+    )(first, shifts, spec, table)
+
+
+def fetch_body(source, out, sem):
+    copy = pltpu.make_async_copy(source, out, sem)
+    copy.start()
+    copy.wait()
+
+
+def fetched(table):
+    return pl.pallas_call(
+        fetch_body,
+        in_specs=[pl.BlockSpec(memory_space=pl.ANY)],
+        out_specs=pl.BlockSpec(memory_space=pltpu.VMEM),
+        out_shape=jax.ShapeDtypeStruct(table.shape, table.dtype),
+        scratch_shapes=[pltpu.SemaphoreType.DMA],
+        compiler_params=pltpu.CompilerParams(vmem_limit_bytes=16 * MIB),
+        name="fetch_table",
+    )(table)
 
 
 def take_cells(spots, field, into, base, slots):
@@ -165,35 +194,31 @@
     return total.T
 
 
-def above_body(slots, pos, coefs, table, field, above_out, into):
-    step = pl.program_id(0)
+def above_body(slots, tiles, spots, coefs, table, field, above_out, into):
     sources, rows, width = coefs.shape
     own = rows // PD
     span = own + 1
     pitch = FIELD_PLANES * span
-
-    @pl.when(step == 0)
-    def _():
-        blank = jnp.zeros((PD * span, 128), F32)
-        for t in range(FIELD_TILES):
-            field[pl.ds(t * pitch, PD * span), :] = blank
-            field[pl.ds(t * pitch + 2 * PD * span, (PD - 1) * span), :] = blank[span:]
-        field[pl.ds((FIELD_TILES - 1) * pitch + PD * span, PD * span), :] = blank
-
+    blank = jnp.zeros((PD * span, 128), F32)
+    for t in range(FIELD_TILES):
+        field[pl.ds(t * pitch, PD * span), :] = blank
+        field[pl.ds(t * pitch + 2 * PD * span, (PD - 1) * span), :] = blank[span:]
+    field[pl.ds((FIELD_TILES - 1) * pitch + PD * span, PD * span), :] = blank
     left = jnp.concatenate([coefs[j] for j in range(sources)], axis=1)
-    velocity = jnp.dot(left, table[...], preferred_element_type=F32)
-    parts = velocity.shape[1] // 128
-    for j in range(parts):
-        for x in range(PD):
-            start = (parts * step + j) * pitch + (PD + x) * span
-            field[pl.ds(start, own), :] = velocity[
-                x * own : (x + 1) * own, j * 128 : (j + 1) * 128
-            ]
-
-    @pl.when(step == pl.num_programs(0) - 1)
-    def _():
-        take_cells(pos, field, into, 2 * slots, slots)
-        above_out[...] = cells_first(into, slots)[PZ : PD * PZ]
+    size = table.shape[1] // tiles
+    parts = size // 128
+    for t in range(tiles):
+        velocity = jnp.dot(
+            left, table[:, t * size : (t + 1) * size], preferred_element_type=F32
+        )
+        for j in range(parts):
+            for x in range(PD):
+                start = (parts * t + j) * pitch + (PD + x) * span
+                field[pl.ds(start, own), :] = velocity[
+                    x * own : (x + 1) * own, j * 128 : (j + 1) * 128
+                ]
+    take_cells(spots, field, into, 2 * slots, slots)
+    above_out[...] = cells_first(into, slots)[PZ : PD * PZ]
 
 
 def patch_spots(positions, behind, own):
@@ -212,32 +237,23 @@
     own_out[...] = cells_first(into, slots)[: PD * PZ]
 
 
-def above_cells(pos, coefs, table, slots, steps=2):
-    sources, rows, width = coefs.shape
-    length = table.shape[1]
+def above_cells(spots, coefs, table, slots, tiles=2):
+    rows = coefs.shape[1]
     span = rows // PD + 1
-    tile = length // steps
     field_shape = (FIELD_TILES * FIELD_PLANES * span, 128)
+    whole = pl.BlockSpec(memory_space=pltpu.VMEM)
     return pl.pallas_call(
-        functools.partial(above_body, slots),
-        grid=(steps,),
-        in_specs=[
-            pl.BlockSpec(memory_space=pltpu.SMEM),
-            pl.BlockSpec((sources, rows, width), lambda i: (0, 0, 0)),
-            pl.BlockSpec((sources * width, tile), lambda i: (0, i)),
-        ],
-        out_specs=[
-            pl.BlockSpec(field_shape, lambda i: (0, 0)),
-            pl.BlockSpec(((PD - 1) * PZ, slots), lambda i: (0, 0)),
-        ],
+        functools.partial(above_body, slots, tiles),
+        in_specs=[pl.BlockSpec(memory_space=pltpu.SMEM), whole, whole],
+        out_specs=[whole, whole],
         out_shape=[
             jax.ShapeDtypeStruct(field_shape, F32),
             jax.ShapeDtypeStruct(((PD - 1) * PZ, slots), F32),
         ],
         scratch_shapes=[pltpu.VMEM((slots * PITCH, 128), F32)],
-        compiler_params=pltpu.CompilerParams(vmem_limit_bytes=VMEM_MIB * MIB),
+        compiler_params=pltpu.CompilerParams(vmem_limit_bytes=24 * MIB),
         name="above_cells",
-    )(pos, coefs, table)
+    )(spots, coefs, table)
 
 
 def own_cells(pos, field, slots):
@@ -250,7 +266,7 @@
         out_specs=pl.BlockSpec(memory_space=pltpu.VMEM),
         out_shape=jax.ShapeDtypeStruct((PD * PZ, slots), F32),
         scratch_shapes=[pltpu.VMEM((slots * PITCH, 128), F32)],
-        compiler_params=pltpu.CompilerParams(vmem_limit_bytes=48 * MIB),
+        compiler_params=pltpu.CompilerParams(vmem_limit_bytes=24 * MIB),
         name="own_cells",
     )(pos, field)
 
@@ -384,7 +400,7 @@
 
 def back_body(
     length, unroll, tiles,
-    scal, spread, turn, lanes_of, table, spec, out,
+    first, shifts, spread, turn, lanes_of, table, spec, out,
     merged, basis, table_in, spec_in, out_from, sems, out_sems,
 ):
     planes, rows, width = spec_in.shape
@@ -400,7 +416,7 @@
 
     def body(i, carry):
         parts = [spread[i * unroll + u] for u in range(unroll)]
-        kept = merge_sources(length, scal[0], parts, turn[...], own, planes, width)
+        kept = merge_sources(length, first[0], parts, turn[...], own, planes, width)
         for u in range(unroll):
             base = pl.multiple_of((i * unroll + u) * own, own)
             for x in range(planes):
@@ -420,12 +436,12 @@
         span = pl.ds(t * tile, tile)
         mixed = jnp.dot(table_in[span, :], basis[...], preferred_element_type=F32)
         across = t * tile + lax.broadcasted_iota(jnp.int32, (tile, width), 0)
-        along = scal[0] + lax.broadcasted_iota(jnp.int32, (tile, width), 1) // 2
+        along = first[0] + lax.broadcasted_iota(jnp.int32, (tile, width), 1) // 2
         across_norm = jnp.minimum(across, rows - across).astype(F32) * (2.0 / rows)
         along_norm = jnp.minimum(along, length - along).astype(F32) * (2.0 / length)
         factor = 1.0 / (1.0 + across_norm * across_norm + along_norm * along_norm)
         for x in range(planes):
-            cosine, sines = plane_phase(scal[1 + x], scal[0], width, length)
+            cosine, sines = plane_phase(shifts[x], first[0], width, length)
             values = spec_in[x, span, :]
             phased = values * cosine + rotate(values) * sines
             out_from[x, span, :] = factor * (phased + mixed[:, x * width : (x + 1) * width])
@@ -436,14 +452,15 @@
         store.wait()
 
 
-def back_rows(scal, spread, turn, table, spec, length, unroll=8, tiles=4):
+def back_rows(first, shifts, spread, turn, table, spec, length, unroll=8, tiles=4):
     planes, rows, width = spec.shape
     lanes_of = jnp.asarray(lane_table(width))
+    small = pl.BlockSpec(memory_space=pltpu.SMEM)
     whole = pl.BlockSpec(memory_space=pltpu.VMEM)
     away = pl.BlockSpec(memory_space=pl.ANY)
     return pl.pallas_call(
         functools.partial(back_body, length, unroll, tiles),
-        in_specs=[pl.BlockSpec(memory_space=pltpu.SMEM), whole, whole, whole, away, away],
+        in_specs=[small, small, whole, whole, whole, away, away],
         out_specs=away,
         out_shape=jax.ShapeDtypeStruct((planes, rows, width), F32),
         scratch_shapes=[
@@ -457,7 +474,7 @@
         ],
         compiler_params=pltpu.CompilerParams(vmem_limit_bytes=VMEM_MIB * MIB),
         name="back_rows",
-    )(scal, spread, turn, lanes_of, table, spec)
+    )(first, shifts, spread, turn, lanes_of, table, spec)
 
 
 def one_slab_on(value, by):
@@ -472,12 +489,16 @@
     length = width // 2 * pencils
     slots = patch_pos.shape[-1]
     first_wave = (lax.axis_index("pencil") * (width // 2)).astype(jnp.int32)
-    scal = jnp.concatenate([first_wave[None], shear_shift])
+    first = first_wave[None]
     table = jnp.asarray(row_table(rows))
 
     positions = patch_pos[0, 0]
+    coefs = forward_rows(first, shear_shift, spec_vel, table, own, length)
+    positions, wave_table, coefs = lax.optimization_barrier(
+        (positions, jnp.asarray(depth_table(length)), coefs)
+    )
     behind = one_slab_on(positions, 1)
-    coefs = forward_rows(scal, spec_vel, table, own, length)
+    wave_table = fetched(wave_table)
     coefs = coefs.reshape(pencils, planes * own, width)
     here = lax.all_to_all(coefs, "pencil", split_axis=0, concat_axis=0, tiled=True)
     notes = []
@@ -485,10 +506,10 @@
         notes += [held[2] // 32, held[2] % 32, held[0] * own + held[1]]
     notes = jnp.stack(notes + [jnp.zeros_like(notes[0])] * 2).astype(BF16)
     turn = spread_table(first_wave, width, length)
-    here, turn, notes = lax.optimization_barrier((here, turn, notes))
+    here, turn, notes, wave_table = lax.optimization_barrier((here, turn, notes, wave_table))
 
     spots = patch_spots(positions, behind, own)
-    field, above = above_cells(spots, here, jnp.asarray(depth_table(length)), slots)
+    field, above = above_cells(spots, here, wave_table, slots)
     from_above = one_slab_on(above, -1)
     values = own_cells(spots, field, slots)
     forces, spread, upward = marker_forces(
@@ -497,7 +518,7 @@
     from_below = one_slab_on(upward, 1)
     message = jnp.concatenate([spread, from_below, notes])[None]
     gathered = lax.all_gather(message, "pencil", axis=0, tiled=True)
-    new_hat = back_rows(scal, gathered, turn, table, spec_vel, length)
+    new_hat = back_rows(first, shear_shift, gathered, turn, table, spec_vel, length)
     return (new_hat, forces[None, None])
 
 

time: 110 us -> 104 us (0.945)
  Pallas kernels: 31.6 us -> 27.8 us
  waiting for transfers between devices: 30.3 us -> 26.5 us
  local copies, waits for them, and re-layouts: 4.38 us -> 7.46 us
  other arithmetic: 3.1 us -> 1.22 us
    all_to_all x1, waiting for transfers between devices: 25.6 us -> 21.7 us  [shards(): lax.all_to_all(coefs, 'pencil', split_axis=0, concat_axis=0, tiled=True)]
    pallas_call x2 -> x3, Pallas kernels: 14.3 us -> 10.5 us  [the longest x1 6.56 us: forward_rows(): pl.pallas_call(functools.partial(forward_body, length, tiles), in_specs=[...]
    unnamed x15 -> x13, local copies, waits for them, and re-layouts: 4 us -> 7.08 us
    concatenate x1 -> x0, other arithmetic: 1.27 us -> none  [shards(): scal = jnp.concatenate([first_wave[None], shear_shift])]
  transfers between devices with their start and end apart: 4 -> 4, of which waited for: 2 -> 2; matrix products, arithmetic and copies ran while one was open for 3% -> 2% of each run, Pallas kernels for 9% -> 3%
where the time goes in v3:
time: 104 us; the launch traced here: 103 us
  Pallas kernels  27.8 us (27%)
  waiting for transfers between devices  26.5 us (25%)
  blocking collectives  19.9 us (19%)
  starting transfers between devices  18.8 us (18%)
  local copies, waits for them, and re-layouts  7.46 us (7%)
  between operations  1.61 us (2%)
  other arithmetic  1.22 us (1%)
    all_to_all x1, waiting for transfers between devices, shards(): lax.all_to_all(coefs, 'pencil', split_axis=0, concat_axis=0, tiled=True)  21.7 us
    all_gather x1, blocking collectives, shards(): gathered = lax.all_gather(message, 'pencil', axis=0, tiled=True)  19.9 us
    pallas_call x1, Pallas kernels, back_rows(): pl.pallas_call(functools.partial(back_body, length, unroll, tiles), in_sp...  12.8 us
    all_to_all x1, starting transfers between devices, shards(): lax.all_to_all(coefs, 'pencil', split_axis=0, concat_axis=0, tiled=True)  9.44 us
    ppermute x3, starting transfers between devices, one_slab_on(): lax.ppermute(value, 'slab', [(i, i + by) for i in range(size) if 0 <= i +...  9.33 us
    unnamed x13, local copies, waits for them, and re-layouts  7.08 us
    pallas_call x1, Pallas kernels, forward_rows(): pl.pallas_call(functools.partial(forward_body, length, tiles), in_specs=[...  6.56 us
    ppermute x3, waiting for transfers between devices, one_slab_on(): lax.ppermute(value, 'slab', [(i, i + by) for i in range(size) if 0 <= i +...  4.76 us
  transfers between devices with their start and end apart: 4, of which 2 were waited for; matrix products, arithmetic and copies ran while one was open for 2% of the time, Pallas kernels for 3%

profile of v3, /device:TPU:7, one launch (start us, length us, event | category | flops | bytes accessed | tf_op | source)
XLA Modules:
  0.0 103.3 jit_solution(7318410479933151184)
XLA Ops:
  0.6 0.7 copy.21
  1.3 6.6 %forward_rows.1 = bf16[16,4,64,128]{3,2,1,0:T(8,128)(2,1)} custom-call(s32[1]{0:T(128)} %bitcast.first, s32[4]{0:T(128)} %shifts.3, f32[4,1024,128]{2,1,0:T(8,128)} %spec.3, bf16[1024,2048]{1,0:T(8,128)(2,1)} %constant.144.clone.table), custom_call_target="tpu_custom_call" | custom-call | tf_op jit(solution)/shard_map/forward_rows/pallas_call | solution.py:130
  7.9 3.2 %collective-permute-start = (s32[3,256]{1,0:T(4,128)S(1)}, s32[3,256]{1,0:T(4,128)S(1)}, u32[]{:S(2)}, u32[]{:S(2)}) collective-permute-start(s32[3,256]{1,0:T(4,128)S(1)} %bitcast.39), channel_id=1, source_target_pairs={{0,16},{16,32},{32,48},{48,64},{64,80},{80,96},{96,112},{112,128},... | collective-permute-start | bytes 9224 | tf_op jit(solution)/shard_map/ppermute | solution.py:482
  11.1 9.4 %all-to-all-start = ((bf16[16,256,128]{2,1,0:T(8,128)(2,1)}), bf16[16,256,128]{2,1,0:T(8,128)(2,1)S(1)}, u32[]{:S(2)}, u32[]{:S(2)}) async-start(bf16[16,256,128]{2,1,0:T(8,128)(2,1)} %bitcast.33), calls=%async_computation | async-start | bytes 2097152 | tf_op jit(solution)/shard_map/all_to_all | solution.py:503
  20.6 0.1 broadcast_multiply_fusion.1
  20.8 0.2 copy.11
  21.0 0.2 copy.12
  21.2 1.0 pad_maximum_fusion.turn
  22.2 0.0 copy-start.2
  22.2 2.2 %copy-done.2 = bf16[2048,1024]{1,0:T(8,128)(2,1)S(1)} copy-done((bf16[2048,1024]{1,0:T(8,128)(2,1)S(1)}, bf16[2048,1024]{1,0:T(8,128)(2,1)}, u32[]{:S(2)}) %copy-start.2) | copy-done | bytes 4194328
  24.4 0.3 fetch_table.1.table
  24.7 0.0 copy-start
  24.7 1.9 %copy-done = bf16[2048,1024]{1,0:T(8,128)(2,1)} copy-done((bf16[2048,1024]{1,0:T(8,128)(2,1)}, bf16[2048,1024]{1,0:T(8,128)(2,1)S(1)}, u32[]{:S(2)}) %copy-start) | copy-done | bytes 4194328
  26.6 0.0 collective-permute-done
  26.7 21.7 %all-to-all-done.coefs = bf16[16,256,128]{2,1,0:T(8,128)(2,1)S(1)} async-done(((bf16[16,256,128]{2,1,0:T(8,128)(2,1)}), bf16[16,256,128]{2,1,0:T(8,128)(2,1)S(1)}, u32[]{:S(2)}, u32[]{:S(2)}) %all-to-all-start) | async-done | bytes 1048608 | tf_op jit(solution)/shard_map/all_to_all | solution.py:503
  48.5 0.0 copy-start.1
  48.5 2.2 %copy-done.1 = bf16[2048,1024]{1,0:T(8,128)(2,1)S(1)} copy-done((bf16[2048,1024]{1,0:T(8,128)(2,1)S(1)}, bf16[2048,1024]{1,0:T(8,128)(2,1)}, u32[]{:S(2)}) %copy-start.1) | copy-done | bytes 4194328
  50.7 0.0 copy-start.3
  50.7 0.0 copy-start.4
  50.7 3.7 %above_cells.1 = (f32[8775,128]{1,0:T(8,128)S(1)}, f32[48,256]{1,0:T(8,128)S(1)}) custom-call(s32[1024]{0:T(1024)S(1)} %pad_add_fusion.spots.pos, bf16[16,256,128]{2,1,0:T(8,128)(2,1)S(1)} %all-to-all-done.coefs, bf16[2048,1024]{1,0:T(8,128)(2,1)S(1)} %copy-done.1), custom_call_target="tpu_custom_call" | custom-call | tf_op jit(solution)/shard_map/above_cells/pallas_call | solution.py:245
  54.4 4.2 %collective-permute-start.1 = (f32[48,256]{1,0:T(8,128)S(1)}, f32[48,256]{1,0:T(8,128)S(1)}, u32[]{:S(2)}, u32[]{:S(2)}) collective-permute-start(f32[48,256]{1,0:T(8,128)S(1)} %get-tuple-element.20), channel_id=1, source_target_pairs={{16,0},{32,16},{48,32},{64,48},{80,64},{96,80},{112,96},{128,112},... | collective-permute-start | bytes 147464 | tf_op jit(solution)/shard_map/ppermute | solution.py:482
  59.2 2.3 %own_cells.1.own = f32[64,256]{1,0:T(8,128)S(1)} custom-call(s32[1024]{0:T(1024)S(1)} %pad_add_fusion.spots.pos, f32[8775,128]{1,0:T(8,128)S(1)} %get-tuple-element.19.field), custom_call_target="tpu_custom_call" | custom-call | tf_op jit(solution)/shard_map/own_cells/pallas_call | solution.py:260
  61.6 0.0 collective-permute-done.1.above
  61.6 0.0 copy-done.3
  61.6 0.0 copy-done.4
  61.6 2.1 %marker_forces.1 = (f32[64,256]{1,0:T(8,128)}, bf16[64,256]{1,0:T(8,128)(2,1)S(1)}, bf16[48,256]{1,0:T(8,128)(2,1)S(1)}) custom-call(s32[1]{0:T(128)} %bitcast.30.count, bf16[64,64,256]{2,1,0:T(8,128)(2,1)S(1)} %bitcast.31, f32[64,256]{1,0:T(8,128)S(1)} %own_cells.1.own, f32[48,256]{1,0:T(8,128)S(1)} %collective-permute-done.1.above, f32[64,256]{1,0:T(8,128)S(1)} %bitcast.32), custom_call_target="tpu_custom_call" | custom-call | tf_op jit(solution)/shard_map/marker_forces/pallas_call | solution.py:306
  63.6 1.9 %collective-permute-start.2 = (bf16[48,256]{1,0:T(8,128)(2,1)S(1)}, bf16[48,256]{1,0:T(8,128)(2,1)S(1)}, u32[]{:S(2)}, u32[]{:S(2)}) collective-permute-start(bf16[48,256]{1,0:T(8,128)(2,1)S(1)} %get-tuple-element.22), channel_id=1, source_target_pairs={{0,16},{16,32},{32,48},{48,64},{64,80},{80,96},{96,112},{112,128},... | collective-permute-start | bytes 73736 | tf_op jit(solution)/shard_map/ppermute | solution.py:482
  65.6 4.8 %collective-permute-done.2 = bf16[48,256]{1,0:T(8,128)(2,1)S(1)} collective-permute-done((bf16[48,256]{1,0:T(8,128)(2,1)S(1)}, bf16[48,256]{1,0:T(8,128)(2,1)S(1)}, u32[]{:S(2)}, u32[]{:S(2)}) %collective-permute-start.2) | collective-permute-done | bytes 24608 | tf_op jit(solution)/shard_map/ppermute | solution.py:482
  70.3 19.9 %all-gather = bf16[1920,256]{1,0:T(8,128)(2,1)} all-gather(bf16[120,256]{1,0:T(8,128)(2,1)S(1)} %pad_maximum_fusion.1), channel_id=2, replica_groups=mesh['slab'=16,'pencil'=16] {'pencil'}, dimensions={0}, use_global_device_ids=true | all-gather | bytes 1044480 | tf_op jit(solution)/shard_map/all_gather | solution.py:520
  90.2 12.8 %back_rows.1 = f32[4,1024,128]{2,1,0:T(8,128)} custom-call(s32[1]{0:T(128)} %bitcast.first, s32[4]{0:T(128)} %shifts.3, bf16[16,120,256]{2,1,0:T(8,128)(2,1)} %bitcast.34, bf16[896,224]{1,0:T(8,128)(2,1)} %pad_maximum_fusion.turn, bf16[128,256]{1,0:T(8,128)(2,1)} %constant.146.clone.lanes_of, bf16[1024,2048]{1,0:T(8,128)(2,1)} %constant.144.clone.table, ...), custom_call_target="tpu_custom_call" | custom-call | tf_op jit(solution)/shard_map/back_rows/pallas_call | solution.py:461
  (15 shorter events, 0.2 us)
Async XLA Ops:
  7.9 18.7 %collective-permute-start = (s32[3,256]{1,0:T(4,128)S(1)}, s32[3,256]{1,0:T(4,128)S(1)}, u32[]{:S(2)}, u32[]{:S(2)}) collective-permute-start(s32[3,256]{1,0:T(4,128)S(1)} %bitcast.39), channel_id=1, source_target_pairs={{0,16},{16,32},{32,48},{48,64},{64,80},{80,96},{96,112},{112,128},... | collective-permute-start | bytes 9224 | tf_op jit(solution)/shard_map/ppermute | solution.py:482
  11.1 37.4 %all-to-all-start = ((bf16[16,256,128]{2,1,0:T(8,128)(2,1)}), bf16[16,256,128]{2,1,0:T(8,128)(2,1)S(1)}, u32[]{:S(2)}, u32[]{:S(2)}) async-start(bf16[16,256,128]{2,1,0:T(8,128)(2,1)} %bitcast.33), calls=%async_computation | async-start | bytes 2097152 | tf_op jit(solution)/shard_map/all_to_all | solution.py:503
  22.2 2.2 %copy-start.2 = (bf16[2048,1024]{1,0:T(8,128)(2,1)S(1)}, bf16[2048,1024]{1,0:T(8,128)(2,1)}, u32[]{:S(2)}) copy-start(bf16[2048,1024]{1,0:T(8,128)(2,1)} %constant.145.clone.source) | copy-start | bytes 12582916
  24.7 2.0 %copy-start = (bf16[2048,1024]{1,0:T(8,128)(2,1)}, bf16[2048,1024]{1,0:T(8,128)(2,1)S(1)}, u32[]{:S(2)}) copy-start(bf16[2048,1024]{1,0:T(8,128)(2,1)S(1)} %fetch_table.1.table) | copy-start | bytes 12582916
  48.5 2.2 %copy-start.1 = (bf16[2048,1024]{1,0:T(8,128)(2,1)S(1)}, bf16[2048,1024]{1,0:T(8,128)(2,1)}, u32[]{:S(2)}) copy-start(bf16[2048,1024]{1,0:T(8,128)(2,1)} %copy-done) | copy-start | bytes 12582916
  50.7 10.9 %copy-start.3 = (bf16[1,1,64,64,256]{4,3,2,1,0:T(8,128)(2,1)S(1)}, bf16[1,1,64,64,256]{4,3,2,1,0:T(8,128)(2,1)}, u32[]{:S(2)}) copy-start(bf16[1,1,64,64,256]{4,3,2,1,0:T(8,128)(2,1)} %param.13) | copy-start | bytes 6291460
  50.7 10.9 %copy-start.4 = (f32[1,1,64,256]{3,2,1,0:T(8,128)S(1)}, f32[1,1,64,256]{3,2,1,0:T(8,128)}, u32[]{:S(2)}) copy-start(f32[1,1,64,256]{3,2,1,0:T(8,128)} %param.14) | copy-start | bytes 196612
  54.4 7.2 %collective-permute-start.1 = (f32[48,256]{1,0:T(8,128)S(1)}, f32[48,256]{1,0:T(8,128)S(1)}, u32[]{:S(2)}, u32[]{:S(2)}) collective-permute-start(f32[48,256]{1,0:T(8,128)S(1)} %get-tuple-element.20), channel_id=1, source_target_pairs={{16,0},{32,16},{48,32},{64,48},{80,64},{96,80},{112,96},{128,112},... | collective-permute-start | bytes 147464 | tf_op jit(solution)/shard_map/ppermute | solution.py:482
  63.6 6.7 %collective-permute-start.2 = (bf16[48,256]{1,0:T(8,128)(2,1)S(1)}, bf16[48,256]{1,0:T(8,128)(2,1)S(1)}, u32[]{:S(2)}, u32[]{:S(2)}) collective-permute-start(bf16[48,256]{1,0:T(8,128)(2,1)S(1)} %get-tuple-element.22), channel_id=1, source_target_pairs={{0,16},{16,32},{32,48},{48,64},{64,80},{80,96},{96,112},{112,128},... | collective-permute-start | bytes 73736 | tf_op jit(solution)/shard_map/ppermute | solution.py:482

commit v4 on v3

--- a/solution.py
+++ b/solution.py
@@ -146,24 +146,6 @@
     )(first, shifts, spec, table)
 
 
-def fetch_body(source, out, sem):
-    copy = pltpu.make_async_copy(source, out, sem)
-    copy.start()
-    copy.wait()
-
-
-def fetched(table):
-    return pl.pallas_call(
-        fetch_body,
-        in_specs=[pl.BlockSpec(memory_space=pl.ANY)],
-        out_specs=pl.BlockSpec(memory_space=pltpu.VMEM),
-        out_shape=jax.ShapeDtypeStruct(table.shape, table.dtype),
-        scratch_shapes=[pltpu.SemaphoreType.DMA],
-        compiler_params=pltpu.CompilerParams(vmem_limit_bytes=16 * MIB),
-        name="fetch_table",
-    )(table)
-
-
 def take_cells(spots, field, into, base, slots):
     lane = lax.broadcasted_iota(jnp.int32, (8, 128), 1)
     pitch = field.shape[0] // FIELD_TILES
@@ -452,7 +434,7 @@
         store.wait()
 
 
-def back_rows(first, shifts, spread, turn, table, spec, length, unroll=8, tiles=4):
+def back_rows(first, shifts, spread, turn, table, spec, length, unroll=16, tiles=4):
     planes, rows, width = spec.shape
     lanes_of = jnp.asarray(lane_table(width))
     small = pl.BlockSpec(memory_space=pltpu.SMEM)
@@ -494,22 +476,19 @@
 
     positions = patch_pos[0, 0]
     coefs = forward_rows(first, shear_shift, spec_vel, table, own, length)
-    positions, wave_table, coefs = lax.optimization_barrier(
-        (positions, jnp.asarray(depth_table(length)), coefs)
-    )
+    later_wave, coefs = lax.optimization_barrier((first_wave, coefs))
+    turn = spread_table(later_wave, width, length)
+    positions, turn = lax.optimization_barrier((positions, turn))
     behind = one_slab_on(positions, 1)
-    wave_table = fetched(wave_table)
     coefs = coefs.reshape(pencils, planes * own, width)
     here = lax.all_to_all(coefs, "pencil", split_axis=0, concat_axis=0, tiled=True)
     notes = []
     for held in (positions, behind):
         notes += [held[2] // 32, held[2] % 32, held[0] * own + held[1]]
     notes = jnp.stack(notes + [jnp.zeros_like(notes[0])] * 2).astype(BF16)
-    turn = spread_table(first_wave, width, length)
-    here, turn, notes, wave_table = lax.optimization_barrier((here, turn, notes, wave_table))
 
     spots = patch_spots(positions, behind, own)
-    field, above = above_cells(spots, here, wave_table, slots)
+    field, above = above_cells(spots, here, jnp.asarray(depth_table(length)), slots)
     from_above = one_slab_on(above, -1)
     values = own_cells(spots, field, slots)
     forces, spread, upward = marker_forces(

time: 104 us -> 99.8 us (0.960)
  local copies, waits for them, and re-layouts: 7.46 us -> 2.64 us
  waiting for transfers between devices: 26.5 us -> 27.7 us
    unnamed x13 -> x11, local copies, waits for them, and re-layouts: 7.08 us -> 2.26 us
    ppermute x3, waiting for transfers between devices: 4.76 us -> 8.1 us  [one_slab_on(): lax.ppermute(value, 'slab', [(i, i + by) for i in range(size) if 0 <= i +...]
    all_to_all x1, waiting for transfers between devices: 21.7 us -> 19.6 us  [shards(): lax.all_to_all(coefs, 'pencil', split_axis=0, concat_axis=0, tiled=True)]
  transfers between devices with their start and end apart: 4 -> 4, of which waited for: 2 -> 3; matrix products, arithmetic and copies ran while one was open for 2% -> 2% of each run, Pallas kernels for 3% -> 2%
where the time goes in v4:
time: 99.8 us; the launch traced here: 99.5 us
  waiting for transfers between devices  27.7 us (28%)
  Pallas kernels  27.1 us (27%)
  blocking collectives  19.9 us (20%)
  starting transfers between devices  19.2 us (19%)
  local copies, waits for them, and re-layouts  2.64 us (3%)
  between operations  1.61 us (2%)
  other arithmetic  1.23 us (1%)
    all_gather x1, blocking collectives, shards(): gathered = lax.all_gather(message, 'pencil', axis=0, tiled=True)  19.9 us
    all_to_all x1, waiting for transfers between devices, shards(): lax.all_to_all(coefs, 'pencil', split_axis=0, concat_axis=0, tiled=True)  19.6 us
    pallas_call x1, Pallas kernels, back_rows(): pl.pallas_call(functools.partial(back_body, length, unroll, tiles), in_sp...  12.3 us
    ppermute x3, starting transfers between devices, one_slab_on(): lax.ppermute(value, 'slab', [(i, i + by) for i in range(size) if 0 <= i +...  10.1 us
    all_to_all x1, starting transfers between devices, shards(): lax.all_to_all(coefs, 'pencil', split_axis=0, concat_axis=0, tiled=True)  9.17 us
    ppermute x3, waiting for transfers between devices, one_slab_on(): lax.ppermute(value, 'slab', [(i, i + by) for i in range(size) if 0 <= i +...  8.1 us
    pallas_call x1, Pallas kernels, forward_rows(): pl.pallas_call(functools.partial(forward_body, length, tiles), in_specs=[...  6.7 us
    pallas_call x1, Pallas kernels, above_cells(): pl.pallas_call(functools.partial(above_body, slots, tiles), in_specs=[pl....  3.68 us
  transfers between devices with their start and end apart: 4, of which 3 were waited for; matrix products, arithmetic and copies ran while one was open for 2% of the time, Pallas kernels for 2%

profile of v4, /device:TPU:7, one launch (start us, length us, event | category | flops | bytes accessed | tf_op | source)
XLA Modules:
  0.0 99.5 jit_solution(7058682343330600151)
XLA Ops:
  0.6 0.0 copy-start.3
  0.6 6.7 %forward_rows.1 = bf16[16,4,64,128]{3,2,1,0:T(8,128)(2,1)} custom-call(s32[1]{0:T(128)} %bitcast.first, s32[4]{0:T(128)} %shifts.3, f32[4,1024,128]{2,1,0:T(8,128)} %spec.3, bf16[1024,2048]{1,0:T(8,128)(2,1)} %constant.144.clone.table), custom_call_target="tpu_custom_call" | custom-call | tf_op jit(solution)/shard_map/forward_rows/pallas_call | solution.py:130
  7.4 9.2 %all-to-all-start = ((bf16[16,256,128]{2,1,0:T(8,128)(2,1)}), bf16[16,256,128]{2,1,0:T(8,128)(2,1)S(1)}, u32[]{:S(2)}, u32[]{:S(2)}) async-start(bf16[16,256,128]{2,1,0:T(8,128)(2,1)} %bitcast.33), calls=%async_computation | async-start | bytes 2097152 | tf_op jit(solution)/shard_map/all_to_all | solution.py:484
  16.6 0.1 broadcast_multiply_fusion.1
  16.7 0.2 copy.11
  16.9 0.2 copy.12
  17.1 0.0 copy-done.3
  17.1 1.0 pad_maximum_fusion.turn
  18.1 3.2 %collective-permute-start = (s32[3,256]{1,0:T(4,128)S(1)}, s32[3,256]{1,0:T(4,128)S(1)}, u32[]{:S(2)}, u32[]{:S(2)}) collective-permute-start(s32[3,256]{1,0:T(4,128)S(1)} %bitcast.39), channel_id=1, source_target_pairs={{0,16},{16,32},{32,48},{48,64},{64,80},{80,96},{96,112},{112,128},... | collective-permute-start | bytes 9224 | tf_op jit(solution)/shard_map/ppermute | solution.py:464
  21.4 3.3 %collective-permute-done = s32[3,256]{1,0:T(4,128)S(1)} collective-permute-done((s32[3,256]{1,0:T(4,128)S(1)}, s32[3,256]{1,0:T(4,128)S(1)}, u32[]{:S(2)}, u32[]{:S(2)}) %collective-permute-start) | collective-permute-done | bytes 3104 | tf_op jit(solution)/shard_map/ppermute | solution.py:464
  24.8 19.6 %all-to-all-done.coefs = bf16[16,256,128]{2,1,0:T(8,128)(2,1)S(1)} async-done(((bf16[16,256,128]{2,1,0:T(8,128)(2,1)}), bf16[16,256,128]{2,1,0:T(8,128)(2,1)S(1)}, u32[]{:S(2)}, u32[]{:S(2)}) %all-to-all-start) | async-done | bytes 1048608 | tf_op jit(solution)/shard_map/all_to_all | solution.py:484
  44.5 0.0 copy-start
  44.5 2.2 %copy-done = bf16[2048,1024]{1,0:T(8,128)(2,1)S(1)} copy-done((bf16[2048,1024]{1,0:T(8,128)(2,1)S(1)}, bf16[2048,1024]{1,0:T(8,128)(2,1)}, u32[]{:S(2)}) %copy-start) | copy-done | bytes 4194328
  46.6 0.0 copy-start.1
  46.6 0.0 copy-start.2
  46.6 3.7 %above_cells.1 = (f32[8775,128]{1,0:T(8,128)S(1)}, f32[48,256]{1,0:T(8,128)S(1)}) custom-call(s32[1024]{0:T(1024)S(1)} %pad_add_fusion.spots.pos, bf16[16,256,128]{2,1,0:T(8,128)(2,1)S(1)} %all-to-all-done.coefs, bf16[2048,1024]{1,0:T(8,128)(2,1)S(1)} %copy-done), custom_call_target="tpu_custom_call" | custom-call | tf_op jit(solution)/shard_map/above_cells/pallas_call | solution.py:227
  50.3 4.9 %collective-permute-start.1 = (f32[48,256]{1,0:T(8,128)S(1)}, f32[48,256]{1,0:T(8,128)S(1)}, u32[]{:S(2)}, u32[]{:S(2)}) collective-permute-start(f32[48,256]{1,0:T(8,128)S(1)} %get-tuple-element.15), channel_id=1, source_target_pairs={{16,0},{32,16},{48,32},{64,48},{80,64},{96,80},{112,96},{128,112},... | collective-permute-start | bytes 147464 | tf_op jit(solution)/shard_map/ppermute | solution.py:464
  55.9 2.3 %own_cells.1.own = f32[64,256]{1,0:T(8,128)S(1)} custom-call(s32[1024]{0:T(1024)S(1)} %pad_add_fusion.spots.pos, f32[8775,128]{1,0:T(8,128)S(1)} %get-tuple-element.14.field), custom_call_target="tpu_custom_call" | custom-call | tf_op jit(solution)/shard_map/own_cells/pallas_call | solution.py:242
  58.2 0.0 collective-permute-done.1.above
  58.2 0.0 copy-done.1
  58.3 0.0 copy-done.2
  58.3 2.1 %marker_forces.1 = (f32[64,256]{1,0:T(8,128)}, bf16[64,256]{1,0:T(8,128)(2,1)S(1)}, bf16[48,256]{1,0:T(8,128)(2,1)S(1)}) custom-call(s32[1]{0:T(128)} %bitcast.30.count, bf16[64,64,256]{2,1,0:T(8,128)(2,1)S(1)} %bitcast.31, f32[64,256]{1,0:T(8,128)S(1)} %own_cells.1.own, f32[48,256]{1,0:T(8,128)S(1)} %collective-permute-done.1.above, f32[64,256]{1,0:T(8,128)S(1)} %bitcast.32), custom_call_target="tpu_custom_call" | custom-call | tf_op jit(solution)/shard_map/marker_forces/pallas_call | solution.py:288
  60.3 1.9 %collective-permute-start.2 = (bf16[48,256]{1,0:T(8,128)(2,1)S(1)}, bf16[48,256]{1,0:T(8,128)(2,1)S(1)}, u32[]{:S(2)}, u32[]{:S(2)}) collective-permute-start(bf16[48,256]{1,0:T(8,128)(2,1)S(1)} %get-tuple-element.17), channel_id=1, source_target_pairs={{0,16},{16,32},{32,48},{48,64},{64,80},{80,96},{96,112},{112,128},... | collective-permute-start | bytes 73736 | tf_op jit(solution)/shard_map/ppermute | solution.py:464
  62.2 4.8 %collective-permute-done.2 = bf16[48,256]{1,0:T(8,128)(2,1)S(1)} collective-permute-done((bf16[48,256]{1,0:T(8,128)(2,1)S(1)}, bf16[48,256]{1,0:T(8,128)(2,1)S(1)}, u32[]{:S(2)}, u32[]{:S(2)}) %collective-permute-start.2) | collective-permute-done | bytes 24608 | tf_op jit(solution)/shard_map/ppermute | solution.py:464
  67.0 19.9 %all-gather = bf16[1920,256]{1,0:T(8,128)(2,1)} all-gather(bf16[120,256]{1,0:T(8,128)(2,1)S(1)} %concatenate.12), channel_id=2, replica_groups=mesh['slab'=16,'pencil'=16] {'pencil'}, dimensions={0}, use_global_device_ids=true | all-gather | bytes 1044480 | tf_op jit(solution)/shard_map/all_gather | solution.py:499
  87.0 12.3 %back_rows.1 = f32[4,1024,128]{2,1,0:T(8,128)} custom-call(s32[1]{0:T(128)} %bitcast.first, s32[4]{0:T(128)} %shifts.3, bf16[16,120,256]{2,1,0:T(8,128)(2,1)} %bitcast.34, bf16[896,224]{1,0:T(8,128)(2,1)} %pad_maximum_fusion.turn, bf16[128,256]{1,0:T(8,128)(2,1)} %constant.146.clone.lanes_of, bf16[1024,2048]{1,0:T(8,128)(2,1)} %constant.144.clone.table, ...), custom_call_target="tpu_custom_call" | custom-call | tf_op jit(solution)/shard_map/back_rows/pallas_call | solution.py:443
  (15 shorter events, 0.2 us)
Async XLA Ops:
  0.6 16.5 %copy-start.3 = (s32[1,1,3,256]{3,1,2,0:T(1,128)S(1)}, s32[1,1,3,256]{3,1,2,0:T(1,128)}, u32[]{:S(2)}) copy-start(s32[1,1,3,256]{3,1,2,0:T(1,128)} %param.11) | copy-start | bytes 9220
  7.4 37.1 %all-to-all-start = ((bf16[16,256,128]{2,1,0:T(8,128)(2,1)}), bf16[16,256,128]{2,1,0:T(8,128)(2,1)S(1)}, u32[]{:S(2)}, u32[]{:S(2)}) async-start(bf16[16,256,128]{2,1,0:T(8,128)(2,1)} %bitcast.33), calls=%async_computation | async-start | bytes 2097152 | tf_op jit(solution)/shard_map/all_to_all | solution.py:484
  18.1 6.6 %collective-permute-start = (s32[3,256]{1,0:T(4,128)S(1)}, s32[3,256]{1,0:T(4,128)S(1)}, u32[]{:S(2)}, u32[]{:S(2)}) collective-permute-start(s32[3,256]{1,0:T(4,128)S(1)} %bitcast.39), channel_id=1, source_target_pairs={{0,16},{16,32},{32,48},{48,64},{64,80},{80,96},{96,112},{112,128},... | collective-permute-start | bytes 9224 | tf_op jit(solution)/shard_map/ppermute | solution.py:464
  44.5 2.2 %copy-start = (bf16[2048,1024]{1,0:T(8,128)(2,1)S(1)}, bf16[2048,1024]{1,0:T(8,128)(2,1)}, u32[]{:S(2)}) copy-start(bf16[2048,1024]{1,0:T(8,128)(2,1)} %constant.145.clone.table) | copy-start | bytes 12582916
  46.6 11.6 %copy-start.1 = (bf16[1,1,64,64,256]{4,3,2,1,0:T(8,128)(2,1)S(1)}, bf16[1,1,64,64,256]{4,3,2,1,0:T(8,128)(2,1)}, u32[]{:S(2)}) copy-start(bf16[1,1,64,64,256]{4,3,2,1,0:T(8,128)(2,1)} %param.13) | copy-start | bytes 6291460
  46.6 11.6 %copy-start.2 = (f32[1,1,64,256]{3,2,1,0:T(8,128)S(1)}, f32[1,1,64,256]{3,2,1,0:T(8,128)}, u32[]{:S(2)}) copy-start(f32[1,1,64,256]{3,2,1,0:T(8,128)} %param.14) | copy-start | bytes 196612
  50.3 7.9 %collective-permute-start.1 = (f32[48,256]{1,0:T(8,128)S(1)}, f32[48,256]{1,0:T(8,128)S(1)}, u32[]{:S(2)}, u32[]{:S(2)}) collective-permute-start(f32[48,256]{1,0:T(8,128)S(1)} %get-tuple-element.15), channel_id=1, source_target_pairs={{16,0},{32,16},{48,32},{64,48},{80,64},{96,80},{112,96},{128,112},... | collective-permute-start | bytes 147464 | tf_op jit(solution)/shard_map/ppermute | solution.py:464
  60.3 6.7 %collective-permute-start.2 = (bf16[48,256]{1,0:T(8,128)(2,1)S(1)}, bf16[48,256]{1,0:T(8,128)(2,1)S(1)}, u32[]{:S(2)}, u32[]{:S(2)}) collective-permute-start(bf16[48,256]{1,0:T(8,128)(2,1)S(1)} %get-tuple-element.17), channel_id=1, source_target_pairs={{0,16},{16,32},{32,48},{48,64},{64,80},{80,96},{96,112},{112,128},... | collective-permute-start | bytes 73736 | tf_op jit(solution)/shard_map/ppermute | solution.py:464

commit v5 on v4

--- a/solution.py
+++ b/solution.py
@@ -82,13 +82,15 @@
 
 
 def forward_body(
-    length, tiles, first, shifts, spec, table, out,
+    length, tiles, begin, first, shifts, spec, table, out,
     basis, spec_in, table_in, out_from, sems, table_sems, out_sems,
 ):
     planes, rows, width = spec_in.shape
     dests, _, own, _ = out_from.shape
     tile = rows // tiles
-    loads = [pltpu.make_async_copy(spec.at[x], spec_in.at[x], sems.at[x]) for x in range(planes)]
+    loads = [
+        pltpu.make_async_copy(spec.at[begin + x], spec_in.at[x], sems.at[x]) for x in range(planes)
+    ]
     spans = [pl.ds(t * tile, tile) for t in range(tiles)]
     tables = [
         pltpu.make_async_copy(table.at[span, :], table_in.at[span, :], table_sems.at[t])
@@ -98,7 +100,7 @@
         load.start()
     for x in range(planes):
         loads[x].wait()
-        cosine, sines = plane_phase(shifts[x], first[0], width, length)
+        cosine, sines = plane_phase(shifts[begin + x], first[0], width, length)
         values = spec_in[x]
         turned = rotate(values)
         lanes = pl.ds(x * width, width)
@@ -122,19 +124,19 @@
         store.wait()
 
 
-def forward_rows(first, shifts, spec, table, own, length, tiles=2):
-    planes, rows, width = spec.shape
+def forward_rows(first, shifts, spec, table, own, length, begin, planes, tiles=2):
+    _, rows, width = spec.shape
     small = pl.BlockSpec(memory_space=pltpu.SMEM)
     away = pl.BlockSpec(memory_space=pl.ANY)
     shape = (rows // own, planes, own, width)
     return pl.pallas_call(
-        functools.partial(forward_body, length, tiles),
+        functools.partial(forward_body, length, tiles, begin),
         in_specs=[small, small, away, away],
         out_specs=away,
         out_shape=jax.ShapeDtypeStruct(shape, BF16),
         scratch_shapes=[
             pltpu.VMEM((2 * rows, planes * width), BF16),
-            pltpu.VMEM(spec.shape, F32),
+            pltpu.VMEM((planes, rows, width), F32),
             pltpu.VMEM(table.shape, BF16),
             pltpu.VMEM(shape, BF16),
             pltpu.SemaphoreType.DMA((planes,)),
@@ -142,6 +144,11 @@
             pltpu.SemaphoreType.DMA((tiles,)),
         ],
         compiler_params=pltpu.CompilerParams(vmem_limit_bytes=VMEM_MIB * MIB),
+        cost_estimate=pl.CostEstimate(
+            flops=4 * rows * rows * planes * width,
+            bytes_accessed=6 * planes * rows * width + 4 * rows * rows,
+            transcendentals=0,
+        ),
         name="forward_rows",
     )(first, shifts, spec, table)
 
@@ -176,8 +183,9 @@
     return total.T
 
 
-def above_body(slots, tiles, spots, coefs, table, field, above_out, into):
-    sources, rows, width = coefs.shape
+def above_body(slots, tiles, spots, lower, upper, table, field, above_out, into):
+    sources, rows, width = lower.shape
+    rows = 2 * rows
     own = rows // PD
     span = own + 1
     pitch = FIELD_PLANES * span
@@ -186,7 +194,13 @@
         field[pl.ds(t * pitch, PD * span), :] = blank
         field[pl.ds(t * pitch + 2 * PD * span, (PD - 1) * span), :] = blank[span:]
     field[pl.ds((FIELD_TILES - 1) * pitch + PD * span, PD * span), :] = blank
-    left = jnp.concatenate([coefs[j] for j in range(sources)], axis=1)
+    left = jnp.concatenate(
+        [
+            jnp.concatenate([part[j] for j in range(sources)], axis=1)
+            for part in (lower, upper)
+        ],
+        axis=0,
+    )
     size = table.shape[1] // tiles
     parts = size // 128
     for t in range(tiles):
@@ -219,14 +233,14 @@
     own_out[...] = cells_first(into, slots)[: PD * PZ]
 
 
-def above_cells(spots, coefs, table, slots, tiles=2):
-    rows = coefs.shape[1]
+def above_cells(spots, lower, upper, table, slots, tiles=2):
+    rows = 2 * lower.shape[1]
     span = rows // PD + 1
     field_shape = (FIELD_TILES * FIELD_PLANES * span, 128)
     whole = pl.BlockSpec(memory_space=pltpu.VMEM)
     return pl.pallas_call(
         functools.partial(above_body, slots, tiles),
-        in_specs=[pl.BlockSpec(memory_space=pltpu.SMEM), whole, whole],
+        in_specs=[pl.BlockSpec(memory_space=pltpu.SMEM), whole, whole, whole],
         out_specs=[whole, whole],
         out_shape=[
             jax.ShapeDtypeStruct(field_shape, F32),
@@ -235,7 +249,7 @@
         scratch_shapes=[pltpu.VMEM((slots * PITCH, 128), F32)],
         compiler_params=pltpu.CompilerParams(vmem_limit_bytes=24 * MIB),
         name="above_cells",
-    )(spots, coefs, table)
+    )(spots, lower, upper, table)
 
 
 def own_cells(pos, field, slots):
@@ -475,20 +489,26 @@
     table = jnp.asarray(row_table(rows))
 
     positions = patch_pos[0, 0]
-    coefs = forward_rows(first, shear_shift, spec_vel, table, own, length)
-    later_wave, coefs = lax.optimization_barrier((first_wave, coefs))
+    half = planes // 2
+    here = []
+    wave = first
+    for begin in (0, half):
+        coefs = forward_rows(
+            wave, shear_shift, spec_vel, table, own, length, begin, half
+        ).reshape(pencils, half * own, width)
+        wave, coefs = lax.optimization_barrier((wave, coefs))
+        here.append(lax.all_to_all(coefs, "pencil", split_axis=0, concat_axis=0, tiled=True))
+    later_wave = wave[0]
     turn = spread_table(later_wave, width, length)
     positions, turn = lax.optimization_barrier((positions, turn))
     behind = one_slab_on(positions, 1)
-    coefs = coefs.reshape(pencils, planes * own, width)
-    here = lax.all_to_all(coefs, "pencil", split_axis=0, concat_axis=0, tiled=True)
     notes = []
     for held in (positions, behind):
         notes += [held[2] // 32, held[2] % 32, held[0] * own + held[1]]
     notes = jnp.stack(notes + [jnp.zeros_like(notes[0])] * 2).astype(BF16)
 
     spots = patch_spots(positions, behind, own)
-    field, above = above_cells(spots, here, jnp.asarray(depth_table(length)), slots)
+    field, above = above_cells(spots, here[0], here[1], jnp.asarray(depth_table(length)), slots)
     from_above = one_slab_on(above, -1)
     values = own_cells(spots, field, slots)
     forces, spread, upward = marker_forces(

time: 99.8 us -> 114 us (1.14)
  waiting for transfers between devices: 27.7 us -> 33.8 us
  Pallas kernels: 27.1 us -> 32.7 us
  starting transfers between devices: 19.2 us -> 22.7 us
    all_to_all x1 -> x2, waiting for transfers between devices: 19.6 us -> 29 us  [shards(): lax.all_to_all(coefs, 'pencil', split_axis=0, concat_axis=0, tiled=True)]
    pallas_call x1 -> x2, Pallas kernels: 6.7 us -> 12.3 us  [forward_rows(): pl.pallas_call(functools.partial(forward_body, length, tiles, begin), in_...]
    all_to_all x1 -> x2, starting transfers between devices: 9.17 us -> 12.6 us  [shards(): lax.all_to_all(coefs, 'pencil', split_axis=0, concat_axis=0, tiled=True)]
    ppermute x3, waiting for transfers between devices: 8.1 us -> 4.79 us  [one_slab_on(): lax.ppermute(value, 'slab', [(i, i + by) for i in range(size) if 0 <= i +...]
  transfers between devices with their start and end apart: 4 -> 5, of which waited for: 3 -> 3; matrix products, arithmetic and copies ran while one was open for 2% -> 1% of each run, Pallas kernels for 2% -> 2%
where the time goes in v5:
time: 114 us
  waiting for transfers between devices  33.8 us (30%)
  Pallas kernels  32.7 us (29%)
  starting transfers between devices  22.7 us (20%)
  blocking collectives  19.2 us (17%)
  local copies, waits for them, and re-layouts  2.64 us (2%)
  between operations  1.64 us (1%)
  other arithmetic  1.23 us (1%)
    all_to_all x2, waiting for transfers between devices, shards(): lax.all_to_all(coefs, 'pencil', split_axis=0, concat_axis=0, tiled=True)  29 us
    all_gather x1, blocking collectives, shards(): gathered = lax.all_gather(message, 'pencil', axis=0, tiled=True)  19.2 us
    all_to_all x2, starting transfers between devices, shards(): lax.all_to_all(coefs, 'pencil', split_axis=0, concat_axis=0, tiled=True)  12.6 us
    pallas_call x1, Pallas kernels, back_rows(): pl.pallas_call(functools.partial(back_body, length, unroll, tiles), in_sp...  12.3 us
    pallas_call x2, Pallas kernels, forward_rows(): pl.pallas_call(functools.partial(forward_body, length, tiles, begin), in_...  12.3 us
    ppermute x3, starting transfers between devices, one_slab_on(): lax.ppermute(value, 'slab', [(i, i + by) for i in range(size) if 0 <= i +...  10.1 us
    ppermute x3, waiting for transfers between devices, one_slab_on(): lax.ppermute(value, 'slab', [(i, i + by) for i in range(size) if 0 <= i +...  4.79 us
    pallas_call x1, Pallas kernels, above_cells(): pl.pallas_call(functools.partial(above_body, slots, tiles), in_specs=[pl....  3.67 us
  transfers between devices with their start and end apart: 5, of which 3 were waited for; matrix products, arithmetic and copies ran while one was open for 1% of the time, Pallas kernels for 2%

profile of v5, /device:TPU:7, one launch (start us, length us, event | category | flops | bytes accessed | tf_op | source)
XLA Modules:
  0.0 113.9 jit_solution(5698113598238569110)
XLA Ops:
  0.6 6.1 %forward_rows.2 = bf16[16,2,64,128]{3,2,1,0:T(8,128)(2,1)} custom-call(s32[1]{0:T(128)} %bitcast.first, s32[4]{0:T(128)} %shifts.5, f32[4,1024,128]{2,1,0:T(8,128)} %spec.5, bf16[1024,2048]{1,0:T(8,128)(2,1)} %constant.144.clone.table), custom_call_target="tpu_custom_call" | custom-call | flops 1073741824 | bytes 5767168 | tf_op jit(solution)/shard_map/forward_rows/pallas_call | solution.py:132
  6.7 0.0 copy-start.3
  6.7 6.2 %forward_rows.3 = bf16[16,2,64,128]{3,2,1,0:T(8,128)(2,1)} custom-call(s32[1]{0:T(128)} %bitcast.first, s32[4]{0:T(128)} %shifts.5, f32[4,1024,128]{2,1,0:T(8,128)} %spec.5, bf16[1024,2048]{1,0:T(8,128)(2,1)} %constant.144.clone.table), custom_call_target="tpu_custom_call" | custom-call | flops 1073741824 | bytes 5767168 | tf_op jit(solution)/shard_map/forward_rows/pallas_call | solution.py:132
  13.0 9.2 %all-to-all-start.1 = ((bf16[16,128,128]{2,1,0:T(8,128)(2,1)}), bf16[16,128,128]{2,1,0:T(8,128)(2,1)S(1)}, u32[]{:S(2)}, u32[]{:S(2)}) async-start(bf16[16,128,128]{2,1,0:T(8,128)(2,1)} %bitcast.36), calls=%async_computation.1 | async-start | bytes 1048576 | tf_op jit(solution)/shard_map/all_to_all | solution.py:500
  22.2 0.1 broadcast_multiply_fusion.1
  22.3 0.2 copy.11
  22.5 0.2 copy.12
  22.7 0.0 copy-done.3
  22.7 1.0 pad_maximum_fusion.turn
  23.7 3.2 %collective-permute-start = (s32[3,256]{1,0:T(4,128)S(1)}, s32[3,256]{1,0:T(4,128)S(1)}, u32[]{:S(2)}, u32[]{:S(2)}) collective-permute-start(s32[3,256]{1,0:T(4,128)S(1)} %bitcast.41), channel_id=1, source_target_pairs={{0,16},{16,32},{32,48},{48,64},{64,80},{80,96},{96,112},{112,128},... | collective-permute-start | bytes 9224 | tf_op jit(solution)/shard_map/ppermute | solution.py:478
  27.0 12.5 %all-to-all-done.1.upper = bf16[16,128,128]{2,1,0:T(8,128)(2,1)S(1)} async-done(((bf16[16,128,128]{2,1,0:T(8,128)(2,1)}), bf16[16,128,128]{2,1,0:T(8,128)(2,1)S(1)}, u32[]{:S(2)}, u32[]{:S(2)}) %all-to-all-start.1) | async-done | bytes 524320 | tf_op jit(solution)/shard_map/all_to_all | solution.py:500
  39.4 3.5 %all-to-all-start = ((bf16[16,128,128]{2,1,0:T(8,128)(2,1)}), bf16[16,128,128]{2,1,0:T(8,128)(2,1)S(1)}, u32[]{:S(2)}, u32[]{:S(2)}) async-start(bf16[16,128,128]{2,1,0:T(8,128)(2,1)} %bitcast.3), calls=%async_computation | async-start | bytes 1048576 | tf_op jit(solution)/shard_map/all_to_all | solution.py:500
  42.9 0.0 collective-permute-done
  43.0 16.6 %all-to-all-done.lower = bf16[16,128,128]{2,1,0:T(8,128)(2,1)S(1)} async-done(((bf16[16,128,128]{2,1,0:T(8,128)(2,1)}), bf16[16,128,128]{2,1,0:T(8,128)(2,1)S(1)}, u32[]{:S(2)}, u32[]{:S(2)}) %all-to-all-start) | async-done | bytes 524320 | tf_op jit(solution)/shard_map/all_to_all | solution.py:500
  59.6 0.0 copy-start
  59.6 2.2 %copy-done = bf16[2048,1024]{1,0:T(8,128)(2,1)S(1)} copy-done((bf16[2048,1024]{1,0:T(8,128)(2,1)S(1)}, bf16[2048,1024]{1,0:T(8,128)(2,1)}, u32[]{:S(2)}) %copy-start) | copy-done | bytes 4194328
  61.8 0.0 copy-start.1
  61.8 0.0 copy-start.2
  61.8 3.7 %above_cells.1 = (f32[8775,128]{1,0:T(8,128)S(1)}, f32[48,256]{1,0:T(8,128)S(1)}) custom-call(s32[1024]{0:T(1024)S(1)} %pad_add_fusion.spots.pos, bf16[16,128,128]{2,1,0:T(8,128)(2,1)S(1)} %all-to-all-done.lower, bf16[16,128,128]{2,1,0:T(8,128)(2,1)S(1)} %all-to-all-done.1.upper, bf16[2048,1024]{1,0:T(8,128)(2,1)S(1)} %copy-done), custom_call_target="tpu_custom_call" | custom-call | tf_op jit(solution)/shard_map/above_cells/pallas_call | solution.py:241
  65.5 4.9 %collective-permute-start.1 = (f32[48,256]{1,0:T(8,128)S(1)}, f32[48,256]{1,0:T(8,128)S(1)}, u32[]{:S(2)}, u32[]{:S(2)}) collective-permute-start(f32[48,256]{1,0:T(8,128)S(1)} %get-tuple-element.19), channel_id=1, source_target_pairs={{16,0},{32,16},{48,32},{64,48},{80,64},{96,80},{112,96},{128,112},... | collective-permute-start | bytes 147464 | tf_op jit(solution)/shard_map/ppermute | solution.py:478
  71.1 2.3 %own_cells.1.own = f32[64,256]{1,0:T(8,128)S(1)} custom-call(s32[1024]{0:T(1024)S(1)} %pad_add_fusion.spots.pos, f32[8775,128]{1,0:T(8,128)S(1)} %get-tuple-element.18.field), custom_call_target="tpu_custom_call" | custom-call | tf_op jit(solution)/shard_map/own_cells/pallas_call | solution.py:256
  73.4 0.0 collective-permute-done.1.above
  73.4 0.0 copy-done.1
  73.4 0.0 copy-done.2
  73.4 2.1 %marker_forces.1 = (f32[64,256]{1,0:T(8,128)}, bf16[64,256]{1,0:T(8,128)(2,1)S(1)}, bf16[48,256]{1,0:T(8,128)(2,1)S(1)}) custom-call(s32[1]{0:T(128)} %bitcast.32.count, bf16[64,64,256]{2,1,0:T(8,128)(2,1)S(1)} %bitcast.33, f32[64,256]{1,0:T(8,128)S(1)} %own_cells.1.own, f32[48,256]{1,0:T(8,128)S(1)} %collective-permute-done.1.above, f32[64,256]{1,0:T(8,128)S(1)} %bitcast.34), custom_call_target="tpu_custom_call" | custom-call | tf_op jit(solution)/shard_map/marker_forces/pallas_call | solution.py:302
  75.5 1.9 %collective-permute-start.2 = (bf16[48,256]{1,0:T(8,128)(2,1)S(1)}, bf16[48,256]{1,0:T(8,128)(2,1)S(1)}, u32[]{:S(2)}, u32[]{:S(2)}) collective-permute-start(bf16[48,256]{1,0:T(8,128)(2,1)S(1)} %get-tuple-element.21), channel_id=1, source_target_pairs={{0,16},{16,32},{32,48},{48,64},{64,80},{80,96},{96,112},{112,128},... | collective-permute-start | bytes 73736 | tf_op jit(solution)/shard_map/ppermute | solution.py:478
  77.4 4.8 %collective-permute-done.2 = bf16[48,256]{1,0:T(8,128)(2,1)S(1)} collective-permute-done((bf16[48,256]{1,0:T(8,128)(2,1)S(1)}, bf16[48,256]{1,0:T(8,128)(2,1)S(1)}, u32[]{:S(2)}, u32[]{:S(2)}) %collective-permute-start.2) | collective-permute-done | bytes 24608 | tf_op jit(solution)/shard_map/ppermute | solution.py:478
  82.2 19.2 %all-gather = bf16[1920,256]{1,0:T(8,128)(2,1)} all-gather(bf16[120,256]{1,0:T(8,128)(2,1)S(1)} %concatenate.12), channel_id=2, replica_groups=mesh['slab'=16,'pencil'=16] {'pencil'}, dimensions={0}, use_global_device_ids=true | all-gather | bytes 1044480 | tf_op jit(solution)/shard_map/all_gather | solution.py:519
  101.4 12.3 %back_rows.1 = f32[4,1024,128]{2,1,0:T(8,128)} custom-call(s32[1]{0:T(128)} %bitcast.first, s32[4]{0:T(128)} %shifts.5, bf16[16,120,256]{2,1,0:T(8,128)(2,1)} %bitcast.35, bf16[896,224]{1,0:T(8,128)(2,1)} %pad_maximum_fusion.turn, bf16[128,256]{1,0:T(8,128)(2,1)} %constant.146.clone.lanes_of, bf16[1024,2048]{1,0:T(8,128)(2,1)} %constant.144.clone.table, ...), custom_call_target="tpu_custom_call" | custom-call | tf_op jit(solution)/shard_map/back_rows/pallas_call | solution.py:457
  (15 shorter events, 0.2 us)
Async XLA Ops:
  6.7 16.0 %copy-start.3 = (s32[1,1,3,256]{3,1,2,0:T(1,128)S(1)}, s32[1,1,3,256]{3,1,2,0:T(1,128)}, u32[]{:S(2)}) copy-start(s32[1,1,3,256]{3,1,2,0:T(1,128)} %param.11) | copy-start | bytes 9220
  13.0 26.5 %all-to-all-start.1 = ((bf16[16,128,128]{2,1,0:T(8,128)(2,1)}), bf16[16,128,128]{2,1,0:T(8,128)(2,1)S(1)}, u32[]{:S(2)}, u32[]{:S(2)}) async-start(bf16[16,128,128]{2,1,0:T(8,128)(2,1)} %bitcast.36), calls=%async_computation.1 | async-start | bytes 1048576 | tf_op jit(solution)/shard_map/all_to_all | solution.py:500
  23.7 19.2 %collective-permute-start = (s32[3,256]{1,0:T(4,128)S(1)}, s32[3,256]{1,0:T(4,128)S(1)}, u32[]{:S(2)}, u32[]{:S(2)}) collective-permute-start(s32[3,256]{1,0:T(4,128)S(1)} %bitcast.41), channel_id=1, source_target_pairs={{0,16},{16,32},{32,48},{48,64},{64,80},{80,96},{96,112},{112,128},... | collective-permute-start | bytes 9224 | tf_op jit(solution)/shard_map/ppermute | solution.py:478
  39.4 20.2 %all-to-all-start = ((bf16[16,128,128]{2,1,0:T(8,128)(2,1)}), bf16[16,128,128]{2,1,0:T(8,128)(2,1)S(1)}, u32[]{:S(2)}, u32[]{:S(2)}) async-start(bf16[16,128,128]{2,1,0:T(8,128)(2,1)} %bitcast.3), calls=%async_computation | async-start | bytes 1048576 | tf_op jit(solution)/shard_map/all_to_all | solution.py:500
  59.6 2.2 %copy-start = (bf16[2048,1024]{1,0:T(8,128)(2,1)S(1)}, bf16[2048,1024]{1,0:T(8,128)(2,1)}, u32[]{:S(2)}) copy-start(bf16[2048,1024]{1,0:T(8,128)(2,1)} %constant.145.clone.table) | copy-start | bytes 12582916
  61.8 11.6 %copy-start.1 = (bf16[1,1,64,64,256]{4,3,2,1,0:T(8,128)(2,1)S(1)}, bf16[1,1,64,64,256]{4,3,2,1,0:T(8,128)(2,1)}, u32[]{:S(2)}) copy-start(bf16[1,1,64,64,256]{4,3,2,1,0:T(8,128)(2,1)} %param.13) | copy-start | bytes 6291460
  61.8 11.6 %copy-start.2 = (f32[1,1,64,256]{3,2,1,0:T(8,128)S(1)}, f32[1,1,64,256]{3,2,1,0:T(8,128)}, u32[]{:S(2)}) copy-start(f32[1,1,64,256]{3,2,1,0:T(8,128)} %param.14) | copy-start | bytes 196612
  65.5 7.9 %collective-permute-start.1 = (f32[48,256]{1,0:T(8,128)S(1)}, f32[48,256]{1,0:T(8,128)S(1)}, u32[]{:S(2)}, u32[]{:S(2)}) collective-permute-start(f32[48,256]{1,0:T(8,128)S(1)} %get-tuple-element.19), channel_id=1, source_target_pairs={{16,0},{32,16},{48,32},{64,48},{80,64},{96,80},{112,96},{128,112},... | collective-permute-start | bytes 147464 | tf_op jit(solution)/shard_map/ppermute | solution.py:478
  75.5 6.7 %collective-permute-start.2 = (bf16[48,256]{1,0:T(8,128)(2,1)S(1)}, bf16[48,256]{1,0:T(8,128)(2,1)S(1)}, u32[]{:S(2)}, u32[]{:S(2)}) collective-permute-start(bf16[48,256]{1,0:T(8,128)(2,1)S(1)} %get-tuple-element.21), channel_id=1, source_target_pairs={{0,16},{16,32},{32,48},{48,64},{64,80},{80,96},{96,112},{112,128},... | collective-permute-start | bytes 73736 | tf_op jit(solution)/shard_map/ppermute | solution.py:478

commit v6 on v4

--- a/solution.py
+++ b/solution.py
@@ -282,7 +282,7 @@
 
 def marker_forces(count, weights, own, above, target):
     markers, cells, slots = weights.shape
-    steps = 4
+    steps = 2
     tile = markers // steps
     whole = lambda i: (0, 0)
     return pl.pallas_call(

time: 99.8 us -> 99.5 us (level)
  no operation moved by 1% of the time
where the time goes in v6:
time: 99.5 us; the launch traced here: 99.1 us
  waiting for transfers between devices  27.7 us (28%)
  Pallas kernels  26.7 us (27%)
  blocking collectives  19.9 us (20%)
  starting transfers between devices  19.2 us (19%)
  local copies, waits for them, and re-layouts  2.64 us (3%)
  between operations  1.61 us (2%)
  other arithmetic  1.23 us (1%)
    all_gather x1, blocking collectives, shards(): gathered = lax.all_gather(message, 'pencil', axis=0, tiled=True)  19.9 us
    all_to_all x1, waiting for transfers between devices, shards(): lax.all_to_all(coefs, 'pencil', split_axis=0, concat_axis=0, tiled=True)  19.6 us
    pallas_call x1, Pallas kernels, back_rows(): pl.pallas_call(functools.partial(back_body, length, unroll, tiles), in_sp...  12.3 us
    ppermute x3, starting transfers between devices, one_slab_on(): lax.ppermute(value, 'slab', [(i, i + by) for i in range(size) if 0 <= i +...  10.1 us
    all_to_all x1, starting transfers between devices, shards(): lax.all_to_all(coefs, 'pencil', split_axis=0, concat_axis=0, tiled=True)  9.17 us
    ppermute x3, waiting for transfers between devices, one_slab_on(): lax.ppermute(value, 'slab', [(i, i + by) for i in range(size) if 0 <= i +...  8.1 us
    pallas_call x1, Pallas kernels, forward_rows(): pl.pallas_call(functools.partial(forward_body, length, tiles), in_specs=[...  6.7 us
    pallas_call x1, Pallas kernels, above_cells(): pl.pallas_call(functools.partial(above_body, slots, tiles), in_specs=[pl....  3.67 us
  transfers between devices with their start and end apart: 4, of which 3 were waited for; matrix products, arithmetic and copies ran while one was open for 2% of the time, Pallas kernels for 2%

profile of v6, /device:TPU:7, one launch (start us, length us, event | category | flops | bytes accessed | tf_op | source)
XLA Modules:
  0.0 99.1 jit_solution(10010789609904552939)
XLA Ops:
  0.6 0.0 copy-start.3
  0.6 6.7 %forward_rows.1 = bf16[16,4,64,128]{3,2,1,0:T(8,128)(2,1)} custom-call(s32[1]{0:T(128)} %bitcast.first, s32[4]{0:T(128)} %shifts.3, f32[4,1024,128]{2,1,0:T(8,128)} %spec.3, bf16[1024,2048]{1,0:T(8,128)(2,1)} %constant.144.clone.table), custom_call_target="tpu_custom_call" | custom-call | tf_op jit(solution)/shard_map/forward_rows/pallas_call | solution.py:130
  7.4 9.2 %all-to-all-start = ((bf16[16,256,128]{2,1,0:T(8,128)(2,1)}), bf16[16,256,128]{2,1,0:T(8,128)(2,1)S(1)}, u32[]{:S(2)}, u32[]{:S(2)}) async-start(bf16[16,256,128]{2,1,0:T(8,128)(2,1)} %bitcast.33), calls=%async_computation | async-start | bytes 2097152 | tf_op jit(solution)/shard_map/all_to_all | solution.py:484
  16.6 0.1 broadcast_multiply_fusion.1
  16.7 0.2 copy.11
  16.9 0.2 copy.12
  17.1 0.0 copy-done.3
  17.1 1.0 pad_maximum_fusion.turn
  18.1 3.2 %collective-permute-start = (s32[3,256]{1,0:T(4,128)S(1)}, s32[3,256]{1,0:T(4,128)S(1)}, u32[]{:S(2)}, u32[]{:S(2)}) collective-permute-start(s32[3,256]{1,0:T(4,128)S(1)} %bitcast.39), channel_id=1, source_target_pairs={{0,16},{16,32},{32,48},{48,64},{64,80},{80,96},{96,112},{112,128},... | collective-permute-start | bytes 9224 | tf_op jit(solution)/shard_map/ppermute | solution.py:464
  21.4 3.3 %collective-permute-done = s32[3,256]{1,0:T(4,128)S(1)} collective-permute-done((s32[3,256]{1,0:T(4,128)S(1)}, s32[3,256]{1,0:T(4,128)S(1)}, u32[]{:S(2)}, u32[]{:S(2)}) %collective-permute-start) | collective-permute-done | bytes 3104 | tf_op jit(solution)/shard_map/ppermute | solution.py:464
  24.8 19.6 %all-to-all-done.coefs = bf16[16,256,128]{2,1,0:T(8,128)(2,1)S(1)} async-done(((bf16[16,256,128]{2,1,0:T(8,128)(2,1)}), bf16[16,256,128]{2,1,0:T(8,128)(2,1)S(1)}, u32[]{:S(2)}, u32[]{:S(2)}) %all-to-all-start) | async-done | bytes 1048608 | tf_op jit(solution)/shard_map/all_to_all | solution.py:484
  44.5 0.0 copy-start
  44.5 2.2 %copy-done = bf16[2048,1024]{1,0:T(8,128)(2,1)S(1)} copy-done((bf16[2048,1024]{1,0:T(8,128)(2,1)S(1)}, bf16[2048,1024]{1,0:T(8,128)(2,1)}, u32[]{:S(2)}) %copy-start) | copy-done | bytes 4194328
  46.6 0.0 copy-start.1
  46.6 0.0 copy-start.2
  46.6 3.7 %above_cells.1 = (f32[8775,128]{1,0:T(8,128)S(1)}, f32[48,256]{1,0:T(8,128)S(1)}) custom-call(s32[1024]{0:T(1024)S(1)} %pad_add_fusion.spots.pos, bf16[16,256,128]{2,1,0:T(8,128)(2,1)S(1)} %all-to-all-done.coefs, bf16[2048,1024]{1,0:T(8,128)(2,1)S(1)} %copy-done), custom_call_target="tpu_custom_call" | custom-call | tf_op jit(solution)/shard_map/above_cells/pallas_call | solution.py:227
  50.3 4.9 %collective-permute-start.1 = (f32[48,256]{1,0:T(8,128)S(1)}, f32[48,256]{1,0:T(8,128)S(1)}, u32[]{:S(2)}, u32[]{:S(2)}) collective-permute-start(f32[48,256]{1,0:T(8,128)S(1)} %get-tuple-element.15), channel_id=1, source_target_pairs={{16,0},{32,16},{48,32},{64,48},{80,64},{96,80},{112,96},{128,112},... | collective-permute-start | bytes 147464 | tf_op jit(solution)/shard_map/ppermute | solution.py:464
  55.9 2.3 %own_cells.1.own = f32[64,256]{1,0:T(8,128)S(1)} custom-call(s32[1024]{0:T(1024)S(1)} %pad_add_fusion.spots.pos, f32[8775,128]{1,0:T(8,128)S(1)} %get-tuple-element.14.field), custom_call_target="tpu_custom_call" | custom-call | tf_op jit(solution)/shard_map/own_cells/pallas_call | solution.py:242
  58.2 0.0 collective-permute-done.1.above
  58.2 0.0 copy-done.1
  58.3 0.0 copy-done.2
  58.3 1.7 %marker_forces.1 = (f32[64,256]{1,0:T(8,128)}, bf16[64,256]{1,0:T(8,128)(2,1)S(1)}, bf16[48,256]{1,0:T(8,128)(2,1)S(1)}) custom-call(s32[1]{0:T(128)} %bitcast.30.count, bf16[64,64,256]{2,1,0:T(8,128)(2,1)S(1)} %bitcast.31, f32[64,256]{1,0:T(8,128)S(1)} %own_cells.1.own, f32[48,256]{1,0:T(8,128)S(1)} %collective-permute-done.1.above, f32[64,256]{1,0:T(8,128)S(1)} %bitcast.32), custom_call_target="tpu_custom_call" | custom-call | tf_op jit(solution)/shard_map/marker_forces/pallas_call | solution.py:288
  60.0 1.9 %collective-permute-start.2 = (bf16[48,256]{1,0:T(8,128)(2,1)S(1)}, bf16[48,256]{1,0:T(8,128)(2,1)S(1)}, u32[]{:S(2)}, u32[]{:S(2)}) collective-permute-start(bf16[48,256]{1,0:T(8,128)(2,1)S(1)} %get-tuple-element.17), channel_id=1, source_target_pairs={{0,16},{16,32},{32,48},{48,64},{64,80},{80,96},{96,112},{112,128},... | collective-permute-start | bytes 73736 | tf_op jit(solution)/shard_map/ppermute | solution.py:464
  61.9 4.8 %collective-permute-done.2 = bf16[48,256]{1,0:T(8,128)(2,1)S(1)} collective-permute-done((bf16[48,256]{1,0:T(8,128)(2,1)S(1)}, bf16[48,256]{1,0:T(8,128)(2,1)S(1)}, u32[]{:S(2)}, u32[]{:S(2)}) %collective-permute-start.2) | collective-permute-done | bytes 24608 | tf_op jit(solution)/shard_map/ppermute | solution.py:464
  66.7 19.9 %all-gather = bf16[1920,256]{1,0:T(8,128)(2,1)} all-gather(bf16[120,256]{1,0:T(8,128)(2,1)S(1)} %concatenate.12), channel_id=2, replica_groups=mesh['slab'=16,'pencil'=16] {'pencil'}, dimensions={0}, use_global_device_ids=true | all-gather | bytes 1044480 | tf_op jit(solution)/shard_map/all_gather | solution.py:499
  86.6 12.3 %back_rows.1 = f32[4,1024,128]{2,1,0:T(8,128)} custom-call(s32[1]{0:T(128)} %bitcast.first, s32[4]{0:T(128)} %shifts.3, bf16[16,120,256]{2,1,0:T(8,128)(2,1)} %bitcast.34, bf16[896,224]{1,0:T(8,128)(2,1)} %pad_maximum_fusion.turn, bf16[128,256]{1,0:T(8,128)(2,1)} %constant.146.clone.lanes_of, bf16[1024,2048]{1,0:T(8,128)(2,1)} %constant.144.clone.table, ...), custom_call_target="tpu_custom_call" | custom-call | tf_op jit(solution)/shard_map/back_rows/pallas_call | solution.py:443
  (15 shorter events, 0.2 us)
Async XLA Ops:
  0.6 16.5 %copy-start.3 = (s32[1,1,3,256]{3,1,2,0:T(1,128)S(1)}, s32[1,1,3,256]{3,1,2,0:T(1,128)}, u32[]{:S(2)}) copy-start(s32[1,1,3,256]{3,1,2,0:T(1,128)} %param.11) | copy-start | bytes 9220
  7.4 37.1 %all-to-all-start = ((bf16[16,256,128]{2,1,0:T(8,128)(2,1)}), bf16[16,256,128]{2,1,0:T(8,128)(2,1)S(1)}, u32[]{:S(2)}, u32[]{:S(2)}) async-start(bf16[16,256,128]{2,1,0:T(8,128)(2,1)} %bitcast.33), calls=%async_computation | async-start | bytes 2097152 | tf_op jit(solution)/shard_map/all_to_all | solution.py:484
  18.1 6.6 %collective-permute-start = (s32[3,256]{1,0:T(4,128)S(1)}, s32[3,256]{1,0:T(4,128)S(1)}, u32[]{:S(2)}, u32[]{:S(2)}) collective-permute-start(s32[3,256]{1,0:T(4,128)S(1)} %bitcast.39), channel_id=1, source_target_pairs={{0,16},{16,32},{32,48},{48,64},{64,80},{80,96},{96,112},{112,128},... | collective-permute-start | bytes 9224 | tf_op jit(solution)/shard_map/ppermute | solution.py:464
  44.5 2.2 %copy-start = (bf16[2048,1024]{1,0:T(8,128)(2,1)S(1)}, bf16[2048,1024]{1,0:T(8,128)(2,1)}, u32[]{:S(2)}) copy-start(bf16[2048,1024]{1,0:T(8,128)(2,1)} %constant.145.clone.table) | copy-start | bytes 12582916
  46.6 11.6 %copy-start.1 = (bf16[1,1,64,64,256]{4,3,2,1,0:T(8,128)(2,1)S(1)}, bf16[1,1,64,64,256]{4,3,2,1,0:T(8,128)(2,1)}, u32[]{:S(2)}) copy-start(bf16[1,1,64,64,256]{4,3,2,1,0:T(8,128)(2,1)} %param.13) | copy-start | bytes 6291460
  46.6 11.6 %copy-start.2 = (f32[1,1,64,256]{3,2,1,0:T(8,128)S(1)}, f32[1,1,64,256]{3,2,1,0:T(8,128)}, u32[]{:S(2)}) copy-start(f32[1,1,64,256]{3,2,1,0:T(8,128)} %param.14) | copy-start | bytes 196612
  50.3 7.9 %collective-permute-start.1 = (f32[48,256]{1,0:T(8,128)S(1)}, f32[48,256]{1,0:T(8,128)S(1)}, u32[]{:S(2)}, u32[]{:S(2)}) collective-permute-start(f32[48,256]{1,0:T(8,128)S(1)} %get-tuple-element.15), channel_id=1, source_target_pairs={{16,0},{32,16},{48,32},{64,48},{80,64},{96,80},{112,96},{128,112},... | collective-permute-start | bytes 147464 | tf_op jit(solution)/shard_map/ppermute | solution.py:464
  60.0 6.7 %collective-permute-start.2 = (bf16[48,256]{1,0:T(8,128)(2,1)S(1)}, bf16[48,256]{1,0:T(8,128)(2,1)S(1)}, u32[]{:S(2)}, u32[]{:S(2)}) collective-permute-start(bf16[48,256]{1,0:T(8,128)(2,1)S(1)} %get-tuple-element.17), channel_id=1, source_target_pairs={{0,16},{16,32},{32,48},{48,64},{64,80},{80,96},{96,112},{112,128},... | collective-permute-start | bytes 73736 | tf_op jit(solution)/shard_map/ppermute | solution.py:464
